TPU v7x, 32 devices: a whole 2x2x4 slice. The times are simulated.
32 devices in a mesh: pipe: 2 (over core), expert: 16 (over z, y, x).
Axes of the slice: x: 2, y: 2, z: 4, core: 2. Of those that a mesh axis runs over, the one named last changes fastest.
Arguments:
- act_a: bfloat16 [2, 1024, 3584], P('pipe', 'expert'), may hold values from -6 to 6
- ids_a: int32 [2, 1024, 2], P('pipe', 'expert'), may hold values from 0 to 3, all different within a row; in each aligned block of 64 rows (0 to 63, 64 to 127, ..., all dimensions but the last counted through in order) at most 40 rows name the same one
- act_b: bfloat16 [2, 1024, 3584], P('pipe', 'expert'), may hold values from -6 to 6
- cot_b: bfloat16 [2, 1024, 3584], P('pipe', 'expert'), may hold values from -6 to 6
- ids_b: int32 [2, 1024, 2], P('pipe', 'expert'), may hold values from 0 to 3, all different within a row; in each aligned block of 64 rows (0 to 63, 64 to 127, ..., all dimensions but the last counted through in order) at most 40 rows name the same one
- norm_gain: bfloat16 [2, 3584], P('pipe'), may hold values from 0.5 to 1.5
- router: bfloat16 [2, 3584, 4], P('pipe'), may hold values from -0.09375 to 0.09375
- w_gate: bfloat16 [2, 16, 3584, 256], P('pipe', 'expert'), may hold values from -0.09375 to 0.09375
- w_up: bfloat16 [2, 16, 3584, 256], P('pipe', 'expert'), may hold values from -0.09375 to 0.09375
- w_down: bfloat16 [2, 16, 256, 3584], P('pipe', 'expert'), may hold values from -0.1875 to 0.1875
Outputs:
- next_a: bfloat16 [2, 1024, 3584], P('pipe', 'expert')
- next_b: bfloat16 [2, 1024, 3584], P('pipe', 'expert')
Inputs may be any that keep to these rules, and one draw needn't show every extreme that they name: `ids_a`: each row names 2 different experts. Within the 64 rows of one device (aligned blocks along the relay and token dimensions taken together) no expert is named by more than 40 rows, a bound that some block reaches of them. `ids_b`: as for ids_a.
All inputs are finite; a program needn't handle non-finite values.
Results may differ from a plain program's by a relative error of at most 0.013.
Values may be sent and summed in bfloat16 or wider, within the bound.
A program may use at most 128 MiB of HBM per device.

v0:
```python
import jax
import jax.numpy as jnp
from jax import lax
from jax.sharding import PartitionSpec as P

SPLIT = 4


route_scale = 2.5
norm_eps = 1e-06


def from_behind(array, axis, by):
    size = lax.axis_size(axis)
    return lax.ppermute(array, axis, [(i, (i + by) % size) for i in range(size)])


def normalize(inputs, gain_row):
    values = inputs.astype(jnp.float32)
    inverse = lax.rsqrt(jnp.mean(values * values, axis=-1, keepdims=True) + norm_eps)
    normed = (values * inverse * gain_row.astype(jnp.float32)).astype(jnp.bfloat16)
    return (normed, values, inverse)


def route_gates(normed, router_cols, expert_ids):
    logits = jnp.dot(normed, router_cols, preferred_element_type=jnp.float32)
    picker = (
        expert_ids[:, :, None] == jnp.arange(router_cols.shape[1], dtype=jnp.int32)[None, None, :]
    )
    chosen = jnp.sum(jnp.where(picker, logits[:, None, :], 0.0), axis=2)
    scores = jax.nn.sigmoid(chosen)
    return (scores, scores / jnp.sum(scores, axis=1, keepdims=True), picker)


def expert_forward(rows_in, gate_w, up_w, down_w):
    gate_pre = jnp.dot(rows_in, gate_w, preferred_element_type=jnp.float32)
    up_pre = jnp.dot(rows_in, up_w, preferred_element_type=jnp.float32)
    sig_gate = jax.nn.sigmoid(gate_pre)
    activation = (gate_pre * sig_gate * up_pre).astype(jnp.bfloat16)
    output = jnp.dot(activation, down_w, preferred_element_type=jnp.float32).astype(jnp.bfloat16)
    return (output, gate_pre, up_pre, sig_gate)


def expert_backward(rows_in, grad_rows, gate_w, up_w, down_w):
    output, gate_pre, up_pre, sig_gate = expert_forward(rows_in, gate_w, up_w, down_w)
    contract = jnp.sum(grad_rows.astype(jnp.float32) * output.astype(jnp.float32), axis=-1).astype(
        jnp.bfloat16
    )
    last_dims = (((1,), (1,)), ((), ()))
    grad_act = lax.dot_general(grad_rows, down_w, last_dims, preferred_element_type=jnp.float32)
    grad_gate = (grad_act * up_pre * sig_gate * (1.0 + gate_pre * (1.0 - sig_gate))).astype(
        jnp.bfloat16
    )
    grad_up = (grad_act * gate_pre * sig_gate).astype(jnp.bfloat16)
    grad_in = lax.dot_general(grad_gate, gate_w, last_dims, preferred_element_type=jnp.float32)
    grad_in = grad_in + lax.dot_general(
        grad_up, up_w, last_dims, preferred_element_type=jnp.float32
    )
    return (grad_in.astype(jnp.bfloat16), contract)


def slot_table(expert_ids, experts):
    flat_ids = expert_ids.reshape(-1)
    onehot = (flat_ids[:, None] == jnp.arange(experts, dtype=jnp.int32)[None, :]).astype(jnp.int32)
    before = jnp.cumsum(onehot, axis=0) - onehot
    return (flat_ids, jnp.sum(before * onehot, axis=1))


def pack_rows(source, flat_ids, slot_index, experts, capacity):
    top_count = flat_ids.shape[0] // source.shape[0]
    token_rows = jnp.arange(flat_ids.shape[0], dtype=jnp.int32) // top_count
    buffer = jnp.zeros((experts, capacity, source.shape[-1]), source.dtype)
    buffer = buffer.at[flat_ids, slot_index].set(source[token_rows])
    return jnp.repeat(buffer, SPLIT, axis=0)


def slice_total(returned, experts, capacity):
    shaped = returned.reshape((experts, SPLIT, capacity) + returned.shape[2:])
    return jnp.sum(shaped.astype(jnp.float32), axis=1)


def per_device(act_a, ids_a, act_b, cot_b, ids_b, norm_gain, router, w_gate, w_up, w_down):
    experts = lax.axis_size("expert") // SPLIT
    token_count = act_a.shape[1]
    top_count = ids_a.shape[2]
    width = act_a.shape[2]
    capacity = min(token_count, max(2, 5 * token_count * top_count // (4 * experts)))
    gain_row = norm_gain[0]
    router_cols = router[0]
    gate_w = w_gate[0, 0]
    up_w = w_up[0, 0]
    down_w = w_down[0, 0]
    normed_a, values_a, inverse_a = normalize(act_a[0], gain_row)
    scores_a, share_a, picker_a = route_gates(normed_a, router_cols, ids_a[0])
    flat_a, slot_a = slot_table(ids_a[0], experts)
    send_a = pack_rows(normed_a, flat_a, slot_a, experts, capacity)
    grad_out = cot_b[0]
    normed_b, values_b, inverse_b = normalize(act_b[0], gain_row)
    scores_b, share_b, picker_b = route_gates(normed_b, router_cols, ids_b[0])
    flat_b, slot_b = slot_table(ids_b[0], experts)
    send_b = pack_rows(normed_b, flat_b, slot_b, experts, capacity)
    send_grad = pack_rows(grad_out, flat_b, slot_b, experts, capacity)
    received = lax.all_to_all(send_a, "expert", split_axis=0, concat_axis=0, tiled=True)
    output = expert_forward(received.reshape(-1, width), gate_w, up_w, down_w)[0]
    back_a = output.reshape(received.shape)
    home_a = lax.all_to_all(back_a, "expert", split_axis=0, concat_axis=0, tiled=True)
    received = (
        lax.all_to_all(send_b, "expert", split_axis=0, concat_axis=0, tiled=True),
        lax.all_to_all(send_grad, "expert", split_axis=0, concat_axis=0, tiled=True),
    )
    received_rows = received[0]
    grad_in, contract = expert_backward(
        received_rows.reshape(-1, width), received[1].reshape(-1, width), gate_w, up_w, down_w
    )
    back_grad = grad_in.reshape(received_rows.shape)
    back_contract = contract.reshape(received_rows.shape[:2])
    home_grad, home_contract = (
        lax.all_to_all(back_grad, "expert", split_axis=0, concat_axis=0, tiled=True),
        lax.all_to_all(back_contract, "expert", split_axis=0, concat_axis=0, tiled=True),
    )
    summed_a = slice_total(home_a, experts, capacity)
    outputs_a = summed_a[flat_a, slot_a].reshape(token_count, top_count, width)
    mixed_a = jnp.einsum("tk,tkd->td", share_a, outputs_a)
    section_a = (values_a + route_scale * mixed_a).astype(jnp.bfloat16)
    next_a = from_behind(section_a[None], "pipe", 1)
    summed_grad = slice_total(home_grad, experts, capacity)
    summed_contract = slice_total(home_contract, experts, capacity)
    grads_in = summed_grad[flat_b, slot_b].reshape(token_count, top_count, width)
    contracts = summed_contract[flat_b, slot_b].reshape(token_count, top_count)
    branch_b = jnp.einsum("tk,tkd->td", share_b, grads_in)
    grad_share = route_scale * contracts
    grad_scores = (grad_share - jnp.sum(share_b * grad_share, axis=1, keepdims=True)) / jnp.sum(
        scores_b, axis=1, keepdims=True
    )
    grad_logit = grad_scores * scores_b * (1.0 - scores_b)
    dense_grad = jnp.sum(jnp.where(picker_b, grad_logit[:, :, None], 0.0), axis=1).astype(
        jnp.bfloat16
    )
    router_term = lax.dot_general(
        dense_grad, router_cols, (((1,), (1,)), ((), ())), preferred_element_type=jnp.float32
    )
    grad_normed = (route_scale * branch_b + router_term) * gain_row.astype(jnp.float32)
    center = jnp.mean(values_b * grad_normed, axis=-1, keepdims=True)
    grad_values = (
        grad_out.astype(jnp.float32)
        + inverse_b * grad_normed
        - values_b * inverse_b * inverse_b * inverse_b * center
    )
    next_b = from_behind(grad_values.astype(jnp.bfloat16)[None], "pipe", -1)
    return (next_a, next_b)


def solution(mesh):
    return jax.shard_map(
        per_device,
        mesh=mesh,
        in_specs=(
            P("pipe", "expert", None),
            P("pipe", "expert", None),
            P("pipe", "expert", None),
            P("pipe", "expert", None),
            P("pipe", "expert", None),
            P("pipe", None),
            P("pipe", None, None),
            P("pipe", "expert", None, None),
            P("pipe", "expert", None, None),
            P("pipe", "expert", None, None),
        ),
        out_specs=(P("pipe", "expert", None), P("pipe", "expert", None)),
        check_vma=False,
    )
```

profile of v0, /device:TPU:13, one launch (start us, length us, event | category | flops | bytes accessed | tf_op | source)
XLA Modules:
  0.0 615.3 jit_solution(5396015172334256253)
XLA Ops:
  0.7 0.9 copy.39
  1.8 1.2 fusion.37
  3.1 1.2 fusion.43
  4.3 0.8 convert_reduce_fusion.2
  5.5 1.4 fusion.32
  7.0 2.0 gather_fusion.3
  9.1 23.0 %scatter_fusion.2 = bf16[4,40,3584]{2,1,0:T(8,128)(2,1)S(1)} fusion(bf16[4,40,3584]{2,1,0:T(8,128)(2,1)S(1)} %broadcast.239.clone.2, s32[128]{0:T(128)S(1)} %get-tuple-element.4, bf16[128,3584]{1,0:T(8,128)(2,1)} %gather_fusion.3), kind=kCustom, calls=%fused_computation.8 | custom fusion | bytes 2753536 | tf_op jit(solution)/shard_map/scatter | solution.py:73
  32.1 2.5 broadcast_in_dim.40
  34.6 6.7 %all-to-all-start.3 = ((bf16[16,40,3584]{2,1,0:T(8,128)(2,1)}), bf16[16,40,3584]{2,1,0:T(8,128)(2,1)}, u32[]{:S(2)}, u32[]{:S(2)}) async-start(bf16[16,40,3584]{2,1,0:T(8,128)(2,1)} %bitcast.162), calls=%async_computation.3 | async-start | bytes 9175040 | tf_op jit(solution)/shard_map/all_to_all | solution.py:108
  42.0 2.1 gather_fusion
  44.4 23.0 %scatter_fusion = bf16[4,40,3584]{2,1,0:T(8,128)(2,1)S(1)} fusion(bf16[4,40,3584]{2,1,0:T(8,128)(2,1)S(1)} %broadcast.239.clone, s32[128]{0:T(128)S(1)} %get-tuple-element.8, bf16[128,3584]{1,0:T(8,128)(2,1)} %gather_fusion), kind=kCustom, calls=%fused_computation.6 | custom fusion | bytes 2753536 | tf_op jit(solution)/shard_map/scatter | solution.py:73
  67.4 76.7 %all-to-all-done.3 = bf16[16,40,3584]{2,1,0:T(8,128)(2,1)} async-done(((bf16[16,40,3584]{2,1,0:T(8,128)(2,1)}), bf16[16,40,3584]{2,1,0:T(8,128)(2,1)}, u32[]{:S(2)}, u32[]{:S(2)}) %all-to-all-start.3) | async-done | bytes 4587552 | tf_op jit(solution)/shard_map/all_to_all | solution.py:108
  144.1 2.5 broadcast_in_dim.36
  146.6 5.3 all-to-all-start
  151.9 2.1 gather_fusion.2
  154.1 23.0 %scatter_fusion.1 = bf16[4,40,3584]{2,1,0:T(8,128)(2,1)S(1)} fusion(bf16[4,40,3584]{2,1,0:T(8,128)(2,1)S(1)} %broadcast.239.clone.1, s32[128]{0:T(128)S(1)} %get-tuple-element.4, bf16[128,3584]{1,0:T(8,128)(2,1)} %gather_fusion.2), kind=kCustom, calls=%fused_computation.7 | custom fusion | bytes 2753536 | tf_op jit(solution)/shard_map/scatter | solution.py:73
  177.1 76.4 %all-to-all-done = bf16[16,40,3584]{2,1,0:T(8,128)(2,1)} async-done(((bf16[16,40,3584]{2,1,0:T(8,128)(2,1)}), bf16[16,40,3584]{2,1,0:T(8,128)(2,1)}, u32[]{:S(2)}, u32[]{:S(2)}) %all-to-all-start) | async-done | bytes 4587552 | tf_op jit(solution)/shard_map/all_to_all | solution.py:103
  253.6 2.4 broadcast_in_dim.39
  255.9 5.2 all-to-all-start.2
  261.2 4.2 fusion.12
  265.4 4.6 fusion.6
  270.1 4.5 fusion.14
  274.6 88.1 %all-to-all-done.2 = bf16[16,40,3584]{2,1,0:T(8,128)(2,1)} async-done(((bf16[16,40,3584]{2,1,0:T(8,128)(2,1)}), bf16[16,40,3584]{2,1,0:T(8,128)(2,1)}, u32[]{:S(2)}, u32[]{:S(2)}) %all-to-all-start.2) | async-done | bytes 4587552 | tf_op jit(solution)/shard_map/all_to_all | solution.py:109
  362.6 4.6 multiply_reduce_fusion
  367.9 4.8 all-to-all-start.5
  372.8 10.0 %convolution_convert_fusion.1 = bf16[640,3584]{1,0:T(8,128)(2,1)} fusion(bf16[1,1,256,3584]{3,2,1,0:T(8,128)(2,1)} %param.19, bf16[640,3584]{1,0:T(8,128)(2,1)} %bitcast.9, bf16[1,1,3584,256]{3,2,1,0:T(8,128)(2,1)S(1)} %copy-done, f32[640,256]{1,0:T(8,128)} %fusion.14), kind=kOutput, calls=%fused_computation.14 | convolution fusion | flops 2352087040 | bytes 13500416 | tf_op jit(solution)/shard_map/dot_general | solution.py:40
  382.7 6.4 %all-to-all-start.1 = ((bf16[16,40,3584]{2,1,0:T(8,128)(2,1)}), bf16[16,40,3584]{2,1,0:T(8,128)(2,1)}, u32[]{:S(2)}, u32[]{:S(2)}) async-start(bf16[16,40,3584]{2,1,0:T(8,128)(2,1)} %bitcast.167), calls=%async_computation.1 | async-start | bytes 9175040 | tf_op jit(solution)/shard_map/all_to_all | solution.py:106
  389.1 4.4 fusion.2
  393.6 1.5 fusion.10
  395.1 3.6 add_convert_fusion
  398.7 91.8 %all-to-all-done.1 = bf16[16,40,3584]{2,1,0:T(8,128)(2,1)} async-done(((bf16[16,40,3584]{2,1,0:T(8,128)(2,1)}), bf16[16,40,3584]{2,1,0:T(8,128)(2,1)}, u32[]{:S(2)}, u32[]{:S(2)}) %all-to-all-start.1) | async-done | bytes 4587552 | tf_op jit(solution)/shard_map/all_to_all | solution.py:106
  490.5 5.3 all-to-all-start.4
  496.7 1.5 gather_fusion.5
  498.6 3.0 convert_reduce_fusion.1
  501.7 4.5 gather_fusion.1
  506.2 2.3 reshape.295
  508.5 1.1 fusion.87
  509.6 0.9 fusion.58
  510.5 2.0 collective-permute-start
  512.5 84.7 %all-to-all-done.4 = bf16[16,40,3584]{2,1,0:T(8,128)(2,1)} async-done(((bf16[16,40,3584]{2,1,0:T(8,128)(2,1)}), bf16[16,40,3584]{2,1,0:T(8,128)(2,1)}, u32[]{:S(2)}, u32[]{:S(2)}) %all-to-all-start.4) | async-done | bytes 4587552 | tf_op jit(solution)/shard_map/all_to_all | solution.py:118
  597.2 3.0 convert_reduce_fusion
  600.3 4.5 gather_fusion.4
  604.8 2.6 reshape.301
  607.4 1.1 fusion.88
  609.4 1.5 collective-permute-start.1
  610.9 1.4 collective-permute-done.1
  612.3 1.8 copy.57
  614.1 0.8 copy.58
  (68 shorter events, 4.7 us)
Async XLA Ops:
  0.6 264.8 %copy-start = (bf16[1,1,3584,256]{3,2,1,0:T(8,128)(2,1)S(1)}, bf16[1,1,3584,256]{3,2,1,0:T(8,128)(2,1)}, u32[]{:S(2)}) copy-start(bf16[1,1,3584,256]{3,2,1,0:T(8,128)(2,1)} %param.18) | copy-start | bytes 5505028
  34.6 6.7 %copy-start.12 = (s32[1,64,2]{1,2,0:T(2,128)S(1)}, s32[1,64,2]{1,2,0:T(2,128)}, u32[]{:S(2)}) copy-start(s32[1,64,2]{1,2,0:T(2,128)} %param.11) | copy-start | bytes 1540
  34.6 109.5 %all-to-all-start.3 = ((bf16[16,40,3584]{2,1,0:T(8,128)(2,1)}), bf16[16,40,3584]{2,1,0:T(8,128)(2,1)}, u32[]{:S(2)}, u32[]{:S(2)}) async-start(bf16[16,40,3584]{2,1,0:T(8,128)(2,1)} %bitcast.162), calls=%async_computation.3 | async-start | bytes 9175040 | tf_op jit(solution)/shard_map/all_to_all | solution.py:108
  146.6 5.3 copy-start.1
  146.6 106.9 %all-to-all-start = ((bf16[16,40,3584]{2,1,0:T(8,128)(2,1)}), bf16[16,40,3584]{2,1,0:T(8,128)(2,1)}, u32[]{:S(2)}, u32[]{:S(2)}) async-start(bf16[16,40,3584]{2,1,0:T(8,128)(2,1)} %bitcast.163), calls=%async_computation | async-start | bytes 9175040 | tf_op jit(solution)/shard_map/all_to_all | solution.py:103
  255.9 106.7 %all-to-all-start.2 = ((bf16[16,40,3584]{2,1,0:T(8,128)(2,1)}), bf16[16,40,3584]{2,1,0:T(8,128)(2,1)}, u32[]{:S(2)}, u32[]{:S(2)}) async-start(bf16[16,40,3584]{2,1,0:T(8,128)(2,1)} %bitcast.164), calls=%async_computation.2 | async-start | bytes 9175040 | tf_op jit(solution)/shard_map/all_to_all | solution.py:109
  265.4 4.7 copy-start.6
  367.9 14.8 %all-to-all-start.5 = ((bf16[16,1,40]{2,1,0:T(2,128)(2,1)}), bf16[16,1,40]{2,1,0:T(2,128)(2,1)S(1)}, u32[]{:S(2)}, u32[]{:S(2)}) async-start(bf16[16,1,40]{2,1,0:T(2,128)(2,1)} %convert_element_type.158), calls=%async_computation.5 | async-start | bytes 16384 | tf_op jit(solution)/shard_map/all_to_all | solution.py:119
  382.7 107.7 %all-to-all-start.1 = ((bf16[16,40,3584]{2,1,0:T(8,128)(2,1)}), bf16[16,40,3584]{2,1,0:T(8,128)(2,1)}, u32[]{:S(2)}, u32[]{:S(2)}) async-start(bf16[16,40,3584]{2,1,0:T(8,128)(2,1)} %bitcast.167), calls=%async_computation.1 | async-start | bytes 9175040 | tf_op jit(solution)/shard_map/all_to_all | solution.py:106
  389.1 4.4 copy-start.7
  389.1 4.4 copy-start.8
  490.5 5.3 copy-start.4
  490.5 5.3 copy-start.9
  490.5 5.8 copy-start.2
  490.5 6.1 copy-start.11
  490.5 106.7 %all-to-all-start.4 = ((bf16[16,40,3584]{2,1,0:T(8,128)(2,1)}), bf16[16,40,3584]{2,1,0:T(8,128)(2,1)}, u32[]{:S(2)}, u32[]{:S(2)}) async-start(bf16[16,40,3584]{2,1,0:T(8,128)(2,1)} %bitcast.165), calls=%async_computation.4 | async-start | bytes 9175040 | tf_op jit(solution)/shard_map/all_to_all | solution.py:118
  508.5 1.1 copy-start.5
  510.5 100.4 %collective-permute-start = (bf16[1,64,3584]{2,1,0:T(8,128)(2,1)}, bf16[1,64,3584]{2,1,0:T(8,128)(2,1)}, u32[]{:S(2)}, u32[]{:S(2)}) collective-permute-start(bf16[1,64,3584]{2,1,0:T(8,128)(2,1)} %fusion.58), channel_id=1, source_target_pairs={{0,16},{16,0},{1,17},{17,1},{2,18},{18,2},{3,19},{19,3},{4,20},{20... | collective-permute-start | bytes 1376264 | tf_op jit(solution)/shard_map/ppermute | solution.py:15
  607.3 1.1 copy-start.3
  607.4 1.1 copy-start.10
  609.4 2.9 collective-permute-start.1
where the time goes:
time: 625 us; the launch traced here: 615 us
  waiting for transfers between devices  419 us (67%)
  local copies, waits for them, and re-layouts  104 us (17%)
  matrix products  40.8 us (7%)
  starting transfers between devices  37.2 us (6%)
  other arithmetic  13.1 us (2%)
    all_to_all x1, waiting for transfers between devices, per_device(): lax.all_to_all(back_a, 'expert', split_axis=0, concat_axis=0, tiled=True)  91.8 us
    all_to_all x1, waiting for transfers between devices, per_device(): lax.all_to_all(send_grad, 'expert', split_axis=0, concat_axis=0, tiled=True)  88.1 us
    all_to_all x1, waiting for transfers between devices, per_device(): lax.all_to_all(back_grad, 'expert', split_axis=0, concat_axis=0, tiled=True)  84.7 us
    all_to_all x1, waiting for transfers between devices, per_device(): lax.all_to_all(send_b, 'expert', split_axis=0, concat_axis=0, tiled=True)  76.7 us
    all_to_all x1, waiting for transfers between devices, per_device(): lax.all_to_all(send_a, 'expert', split_axis=0, concat_axis=0, tiled=True)  76.4 us
    scatter x3, local copies, waits for them, and re-layouts, pack_rows(): buffer = buffer.at[flat_ids, slot_index].set(source[token_rows])  69.1 us
    dot_general x2, matrix products, expert_forward(): jnp.dot(activation, down_w, preferred_element_type=jnp.float32)  14.6 us
  transfers between devices with their start and end apart: 8, of which 6 were waited for; matrix products, arithmetic and copies ran while one was open for 18% of the time, Pallas kernels for 0%

commit v1 on v0

v1 whole, which is shorter than its diff:
```python
import jax
import jax.numpy as jnp
from jax import lax
from jax.sharding import PartitionSpec as P

SPLIT = 4


route_scale = 2.5
norm_eps = 1e-06
last_dims = (((1,), (1,)), ((), ()))


def dot(left, right):
    return jnp.dot(left, right, preferred_element_type=jnp.float32)


def dot_last(left, right):
    return lax.dot_general(left, right, last_dims, preferred_element_type=jnp.float32)


def from_behind(array, axis, by):
    size = lax.axis_size(axis)
    return lax.ppermute(array, axis, [(i, (i + by) % size) for i in range(size)])


def from_partner(array, bit):
    size = lax.axis_size("expert")
    return lax.ppermute(array, "expert", [(i, i ^ bit) for i in range(size)])


def normalize(inputs, gain_row):
    values = inputs.astype(jnp.float32)
    inverse = lax.rsqrt(jnp.mean(values * values, axis=-1, keepdims=True) + norm_eps)
    normed = (values * inverse * gain_row.astype(jnp.float32)).astype(jnp.bfloat16)
    return (normed, values, inverse)


def route_gates(normed, router_cols, expert_ids):
    logits = dot(normed, router_cols)
    picker = (
        expert_ids[:, :, None] == jnp.arange(router_cols.shape[1], dtype=jnp.int32)[None, None, :]
    )
    chosen = jnp.sum(jnp.where(picker, logits[:, None, :], 0.0), axis=2)
    scores = jax.nn.sigmoid(chosen)
    return (scores, scores / jnp.sum(scores, axis=1, keepdims=True), picker)


def slot_masks(picker, capacity):
    tokens, _, experts = picker.shape
    named = jnp.any(picker, axis=1)
    below = jnp.tril(jnp.ones((tokens, tokens), jnp.bfloat16))
    place = dot(below, named.astype(jnp.bfloat16)).astype(jnp.int32) - 1
    slots = jnp.arange(capacity, dtype=jnp.int32)
    chosen = (place[:, :, None] == slots[None, None, :]) & named[:, :, None]
    by_rank = picker[:, :, :, None] & chosen[:, None]
    pack = chosen.reshape(tokens, experts * capacity).astype(jnp.bfloat16)
    unpack = by_rank.reshape(tokens, picker.shape[1], experts * capacity).astype(jnp.bfloat16)
    return (pack, unpack)


def pack_rows(pack, source, experts):
    packed = lax.dot_general(
        pack, source, (((0,), (0,)), ((), ())), preferred_element_type=jnp.float32
    ).astype(jnp.bfloat16)
    return packed.reshape(experts, -1, source.shape[1])


def swap_experts(blocks):
    size = lax.axis_size("expert")
    experts = size // SPLIT
    mine = lax.axis_index("expert") // SPLIT
    parts = [lax.dynamic_index_in_dim(blocks, mine, 0, keepdims=False)]
    for step in range(1, experts):
        block = lax.dynamic_index_in_dim(blocks, (mine + step) % experts, 0, keepdims=False)
        pairs = [(i, (i + step * SPLIT) % size) for i in range(size)]
        parts.append(lax.ppermute(block, "expert", pairs))
    return parts


def return_experts(parts):
    size = lax.axis_size("expert")
    experts = size // SPLIT
    mine = lax.axis_index("expert") // SPLIT
    home = [parts[0]]
    for step in range(1, experts):
        pairs = [(i, (i - step * SPLIT) % size) for i in range(size)]
        home.append(lax.ppermute(parts[step], "expert", pairs))
    stacked = jnp.stack(home)
    return jnp.roll(stacked, mine, axis=0)


def forward_slice(rows, gate_w, up_w):
    gate_pre = dot(rows, gate_w)
    up_pre = dot(rows, up_w)
    sig_gate = jax.nn.sigmoid(gate_pre)
    activation = (gate_pre * sig_gate * up_pre).astype(jnp.bfloat16)
    return (activation, gate_pre, up_pre, sig_gate)


def backward_slice(rows, grad_rows, gate_w, up_w, down_w):
    activation, gate_pre, up_pre, sig_gate = forward_slice(rows, gate_w, up_w)
    grad_act = dot_last(grad_rows, down_w)
    contract = jnp.sum(activation.astype(jnp.float32) * grad_act, axis=-1, keepdims=True)
    grad_gate = (grad_act * up_pre * sig_gate * (1.0 + gate_pre * (1.0 - sig_gate))).astype(
        jnp.bfloat16
    )
    grad_up = (grad_act * gate_pre * sig_gate).astype(jnp.bfloat16)
    return (dot_last(grad_gate, gate_w) + dot_last(grad_up, up_w), contract)


def per_device(act_a, ids_a, act_b, cot_b, ids_b, norm_gain, router, w_gate, w_up, w_down):
    experts = lax.axis_size("expert") // SPLIT
    token_count = act_a.shape[1]
    top_count = ids_a.shape[2]
    width = act_a.shape[2]
    capacity = min(token_count, max(2, 5 * token_count * top_count // (4 * experts)))
    gain_row = norm_gain[0]
    router_cols = router[0]
    own = (w_gate[0, 0], w_up[0, 0], w_down[0, 0])
    other = tuple(from_partner(w, 1) for w in own)

    normed_a, values_a, inverse_a = normalize(act_a[0], gain_row)
    scores_a, share_a, picker_a = route_gates(normed_a, router_cols, ids_a[0])
    pack_a, unpack_a = slot_masks(picker_a, capacity)
    parts_a = swap_experts(pack_rows(pack_a, normed_a, experts))

    grad_out = cot_b[0]
    normed_b, values_b, inverse_b = normalize(act_b[0], gain_row)
    scores_b, share_b, picker_b = route_gates(normed_b, router_cols, ids_b[0])
    pack_b, unpack_b = slot_masks(picker_b, capacity)
    both_b = jnp.concatenate(
        [pack_rows(pack_b, normed_b, experts), pack_rows(pack_b, grad_out, experts)], axis=1
    )
    parts_b = swap_experts(both_b)

    rows_a = jnp.concatenate(parts_a)
    far_a = from_partner(rows_a, 2)
    rows_b = jnp.concatenate([part[:capacity] for part in parts_b])
    cots_b = jnp.concatenate([part[capacity:] for part in parts_b])
    far_b = from_partner(rows_b, 2)
    far_cots = from_partner(cots_b, 2)

    def forward(rows):
        act_own = forward_slice(rows, own[0], own[1])[0]
        act_other = forward_slice(rows, other[0], other[1])[0]
        return dot(act_own, own[2]) + dot(act_other, other[2])

    def backward(rows, cots):
        first, first_c = backward_slice(rows, cots, *own)
        second, second_c = backward_slice(rows, cots, *other)
        return (first + second, first_c + second_c)

    back_a = from_partner(forward(far_a).astype(jnp.bfloat16), 2)
    out_a = (forward(rows_a) + back_a.astype(jnp.float32)).astype(jnp.bfloat16)
    home_a = return_experts(list(out_a.reshape(experts, capacity, width)))

    far_grad, far_contract = backward(far_b, far_cots)
    back_grad = from_partner(far_grad.astype(jnp.bfloat16), 2)
    back_contract = from_partner(
        jnp.broadcast_to(far_contract, (experts * capacity, 128)).astype(jnp.bfloat16), 2
    )
    near_grad, near_contract = backward(rows_b, cots_b)
    out_grad = (near_grad + back_grad.astype(jnp.float32)).astype(jnp.bfloat16)
    out_contract = (near_contract + back_contract.astype(jnp.float32)).astype(jnp.bfloat16)
    home_grad = return_experts(list(out_grad.reshape(experts, capacity, width)))
    home_contract = return_experts(list(out_contract.reshape(experts, capacity, 128)))

    home_a = home_a.reshape(-1, width)
    mixed_a = sum(share_a[:, k : k + 1] * dot(unpack_a[:, k], home_a) for k in range(top_count))
    section_a = (values_a + route_scale * mixed_a).astype(jnp.bfloat16)
    next_a = from_behind(section_a[None], "pipe", 1)

    home_grad = home_grad.reshape(-1, width)
    home_contract = home_contract.reshape(-1, 128)
    branch_b = sum(share_b[:, k : k + 1] * dot(unpack_b[:, k], home_grad) for k in range(top_count))
    contracts = jnp.concatenate(
        [dot(unpack_b[:, k], home_contract)[:, :1] for k in range(top_count)], axis=1
    )
    grad_share = route_scale * contracts
    grad_scores = (grad_share - jnp.sum(share_b * grad_share, axis=1, keepdims=True)) / jnp.sum(
        scores_b, axis=1, keepdims=True
    )
    grad_logit = grad_scores * scores_b * (1.0 - scores_b)
    dense_grad = jnp.sum(jnp.where(picker_b, grad_logit[:, :, None], 0.0), axis=1).astype(
        jnp.bfloat16
    )
    router_term = dot_last(dense_grad, router_cols)
    grad_normed = (route_scale * branch_b + router_term) * gain_row.astype(jnp.float32)
    center = jnp.mean(values_b * grad_normed, axis=-1, keepdims=True)
    grad_values = (
        grad_out.astype(jnp.float32)
        + inverse_b * grad_normed
        - values_b * inverse_b * inverse_b * inverse_b * center
    )
    next_b = from_behind(grad_values.astype(jnp.bfloat16)[None], "pipe", -1)
    return (next_a, next_b)


def solution(mesh):
    return jax.shard_map(
        per_device,
        mesh=mesh,
        in_specs=(
            P("pipe", "expert", None),
            P("pipe", "expert", None),
            P("pipe", "expert", None),
            P("pipe", "expert", None),
            P("pipe", "expert", None),
            P("pipe", None),
            P("pipe", None, None),
            P("pipe", "expert", None, None),
            P("pipe", "expert", None, None),
            P("pipe", "expert", None, None),
        ),
        out_specs=(P("pipe", "expert", None), P("pipe", "expert", None)),
        check_vma=False,
    )
```

time: 625 us -> 314 us (0.50)
  waiting for transfers between devices: 419 us -> 179 us
  local copies, waits for them, and re-layouts: 104 us -> 12.3 us
  matrix products: 40.8 us -> 75.9 us
  starting transfers between devices: 37.2 us -> 28.1 us
    all_to_all x6 -> x0, waiting for transfers between devices: 418 us -> none  [the longest x1 91.8 us: per_device(): lax.all_to_all(back_a, 'expert', split_axis=0, concat_axis=0, tiled=True)]
    ppermute x0 -> x24, waiting for transfers between devices: none -> 178 us  [the longest x9 82.2 us: from_partner(): return lax.ppermute(array, 'expert', [(i, i ^ bit) for i in range(size)])]
    scatter x3 -> x0, local copies, waits for them, and re-layouts: 69.1 us -> none  [pack_rows(): buffer = buffer.at[flat_ids, slot_index].set(source[token_rows])]
    dot_general x13 -> x42, matrix products: 40.8 us -> 75.9 us  [the longest x26 44.6 us: dot(): return jnp.dot(left, right, preferred_element_type=jnp.float32)]
    all_to_all x6 -> x0, starting transfers between devices: 33.7 us -> none  [the longest x1 6.74 us: per_device(): lax.all_to_all(send_b, 'expert', split_axis=0, concat_axis=0, tiled=True)]
    ppermute x0 -> x24, starting transfers between devices: none -> 27.2 us  [the longest x9 15.2 us: return_experts(): home.append(lax.ppermute(parts[step], 'expert', pairs))]
    gather x6 -> x0, local copies, waits for them, and re-layouts: 16.6 us -> none  [the longest x3 6.16 us: pack_rows(): buffer = buffer.at[flat_ids, slot_index].set(source[token_rows])]
    concatenate x2 -> x5, other arithmetic: 0.02 us -> 7.46 us  [the longest x1 2.69 us: return_experts(): return jnp.roll(stacked, mine, axis=0)]
  transfers between devices with their start and end apart: 8 -> 26, of which waited for: 6 -> 14; matrix products, arithmetic and copies ran while one was open for 18% -> 27% of each run, Pallas kernels for 0% -> 0%
where the time goes in v1:
time: 314 us; the launch traced here: 310 us
  waiting for transfers between devices  179 us (57%)
  matrix products  75.9 us (24%)
  starting transfers between devices  28.1 us (9%)
  other arithmetic  12.6 us (4%)
  local copies, waits for them, and re-layouts  12.3 us (4%)
    ppermute x9, waiting for transfers between devices, from_partner(): return lax.ppermute(array, 'expert', [(i, i ^ bit) for i in range(size)])  82.2 us
    ppermute x6, waiting for transfers between devices, swap_experts(): parts.append(lax.ppermute(block, 'expert', pairs))  64.5 us
    dot_general x26, matrix products, dot(): return jnp.dot(left, right, preferred_element_type=jnp.float32)  44.6 us
    ppermute x9, waiting for transfers between devices, return_experts(): home.append(lax.ppermute(parts[step], 'expert', pairs))  31.2 us
    dot_general x13, matrix products, dot_last(): lax.dot_general(left, right, last_dims, preferred_element_type=jnp.float32)  28.8 us
    ppermute x9, starting transfers between devices, return_experts(): home.append(lax.ppermute(parts[step], 'expert', pairs))  15.2 us
  transfers between devices with their start and end apart: 26, of which 14 were waited for; matrix products, arithmetic and copies ran while one was open for 27% of the time, Pallas kernels for 0%

profile of v1, /device:TPU:13, one launch (start us, length us, event | category | flops | bytes accessed | tf_op | source)
XLA Modules:
  0.0 309.7 jit_solution(15397034082172760130)
XLA Ops:
  3.7 1.5 convolution_convert_fusion
  6.9 1.3 collective-permute-start.12
  11.5 3.2 %collective-permute-start.1 = (bf16[40,3584]{1,0:T(8,128)(2,1)}, bf16[40,3584]{1,0:T(8,128)(2,1)}, u32[]{:S(2)}, u32[]{:S(2)}) collective-permute-start(bf16[40,3584]{1,0:T(8,128)(2,1)} %get-tuple-element.21), channel_id=1, source_target_pairs={{0,8},{1,9},{2,10},{3,11},{4,12},{5,13},{6,14},{7,15},{8,0},{9,1},... | collective-permute-start | bytes 860168 | tf_op jit(solution)/shard_map/ppermute | solution.py:77
  17.2 58.3 %collective-permute-done = bf16[40,3584]{1,0:T(8,128)(2,1)} collective-permute-done((bf16[40,3584]{1,0:T(8,128)(2,1)}, bf16[40,3584]{1,0:T(8,128)(2,1)}, u32[]{:S(2)}, u32[]{:S(2)}) %collective-permute-start) | collective-permute-done | bytes 286752 | tf_op jit(solution)/shard_map/ppermute | solution.py:77
  75.5 6.1 %collective-permute-done.1 = bf16[40,3584]{1,0:T(8,128)(2,1)} collective-permute-done((bf16[40,3584]{1,0:T(8,128)(2,1)}, bf16[40,3584]{1,0:T(8,128)(2,1)}, u32[]{:S(2)}, u32[]{:S(2)}) %collective-permute-start.1) | collective-permute-done | bytes 286752 | tf_op jit(solution)/shard_map/ppermute | solution.py:77
  83.1 1.3 pad_maximum_fusion
  84.9 4.3 %fusion.66 = f32[160,3584]{1,0:T(8,128)} fusion(f32[160,256]{1,0:T(8,128)S(1)} %fusion.137, bf16[1,1,256,3584]{3,2,1,0:T(8,128)(2,1)} %param.21, bf16[160,3584]{1,0:T(8,128)(2,1)S(1)} %pad_maximum_fusion, bf16[1,1,3584,256]{3,2,1,0:T(8,128)(2,1)S(1)} %copy-done.1), kind=kOutput, calls=%fused_computation.142 | convolution fusion | flops 587448320 | bytes 7274496 | tf_op jit(solution)/shard_map/dot_general | solution.py:15
  95.1 1.2 collective-permute-start.16
  96.4 1.8 fusion.115
  100.0 1.9 fusion.133
  101.9 2.1 multiply_reduce_fusion.3
  104.8 2.2 convolution_add_fusion.3
  107.0 9.1 %collective-permute-done.6 = bf16[160,3584]{1,0:T(8,128)(2,1)S(1)} collective-permute-done((bf16[160,3584]{1,0:T(8,128)(2,1)S(1)}, bf16[160,3584]{1,0:T(8,128)(2,1)S(1)}, u32[]{:S(2)}, u32[]{:S(2)}) %collective-permute-start.6) | collective-permute-done | bytes 1146912 | tf_op jit(solution)/shard_map/ppermute | solution.py:29
  117.6 4.7 %fusion.67 = f32[160,3584]{1,0:T(8,128)} fusion(f32[160,256]{1,0:T(8,128)S(1)} %fusion.135, bf16[1,1,256,3584]{3,2,1,0:T(8,128)(2,1)} %param.21, bf16[160,3584]{1,0:T(8,128)(2,1)} %copy-done.5, bf16[1,1,3584,256]{3,2,1,0:T(8,128)(2,1)S(1)} %copy-done.1), kind=kOutput, calls=%fused_computation.143 | convolution fusion | flops 587448320 | bytes 7274496 | tf_op jit(solution)/shard_map/dot_general | solution.py:15
  122.3 18.3 %collective-permute-done.16 = bf16[160,3584]{1,0:T(8,128)(2,1)} collective-permute-done((bf16[160,3584]{1,0:T(8,128)(2,1)}, bf16[160,3584]{1,0:T(8,128)(2,1)}, u32[]{:S(2)}, u32[]{:S(2)}) %collective-permute-start.16) | collective-permute-done | bytes 1146912 | tf_op jit(solution)/shard_map/ppermute | solution.py:29
  140.6 1.7 fusion.112
  142.4 1.9 fusion.130
  144.2 21.0 %collective-permute-done.15 = bf16[160,3584]{1,0:T(8,128)(2,1)} collective-permute-done((bf16[160,3584]{1,0:T(8,128)(2,1)}, bf16[160,3584]{1,0:T(8,128)(2,1)}, u32[]{:S(2)}, u32[]{:S(2)}) %collective-permute-start.15) | collective-permute-done | bytes 1146912 | tf_op jit(solution)/shard_map/ppermute | solution.py:29
  165.2 2.1 multiply_reduce_fusion.1
  168.1 2.2 convolution_add_fusion.1
  170.3 2.3 fusion.172
  172.6 2.3 fusion.173
  174.9 25.4 %collective-permute-done.5 = bf16[256,3584]{1,0:T(8,128)(2,1)} collective-permute-done((bf16[256,3584]{1,0:T(8,128)(2,1)}, bf16[256,3584]{1,0:T(8,128)(2,1)}, u32[]{:S(2)}, u32[]{:S(2)}) %collective-permute-start.5) | collective-permute-done | bytes 1835040 | tf_op jit(solution)/shard_map/ppermute | solution.py:29
  200.3 2.7 multiply_reduce_fusion
  204.0 2.0 fusion.169
  206.0 5.2 %fusion.7 = bf16[160,3584]{1,0:T(8,128)(2,1)} fusion(f32[160,3584]{1,0:T(8,128)} %fusion.67, bf16[256,3584]{1,0:T(8,128)(2,1)} %collective-permute-done.5, f32[160,256]{1,0:T(8,128)S(1)} %fusion.169, bf16[160,3584]{1,0:T(8,128)(2,1)S(1)} %copy-done.6, bf16[3584,256]{1,0:T(8,128)(2,1)} %collective-permute-done.4), kind=kOutput, calls=%fused_computation.13 | convolution fusion | flops 588595200 | bytes 8421376 | tf_op jit(solution)/shard_map/dot_general | solution.py:15
  211.1 1.2 collective-permute-start.7
  212.4 2.4 fusion.71
  214.8 3.3 %fusion.4 = bf16[160,3584]{1,0:T(8,128)(2,1)} fusion(f32[160,3584]{1,0:T(8,128)S(1)} %copy-done.9, f32[160,3584]{1,0:T(8,128)S(1)} %fusion.71, bf16[3584,256]{1,0:T(8,128)(2,1)} %collective-permute-done.3, f32[160,256]{1,0:T(8,128)S(1)} %fusion.173, f32[160,256]{1,0:T(8,128)S(1)} %get-tuple-element.47, f32[160,256]{1,0:T(8,128)S(1)} %fusion.172), kind=kOutput, calls=%fused_computation.10 | convolution fusion | flops 295731200 | bytes 8060928 | tf_op jit(solution)/shard_map/dot_general | solution.py:19
  218.4 2.3 fusion.170
  220.7 2.6 fusion.171
  223.3 2.8 multiply_reduce_fusion.2
  226.1 3.7 %fusion.69 = f32[160,3584]{1,0:T(8,128)} fusion(bf16[3584,256]{1,0:T(8,128)(2,1)} %collective-permute-done.4, f32[160,256]{1,0:T(8,128)S(1)} %get-tuple-element.51, f32[160,256]{1,0:T(8,128)S(1)} %fusion.171), kind=kOutput, calls=%fused_computation.145 | convolution fusion | flops 293847040 | bytes 4456448 | tf_op jit(solution)/shard_map/dot_general | solution.py:19
  229.9 2.8 fusion.168
  233.6 3.2 %collective-permute-start.23 = (bf16[40,128]{1,0:T(8,128)(2,1)S(1)}, bf16[40,128]{1,0:T(8,128)(2,1)S(1)}, u32[]{:S(2)}, u32[]{:S(2)}) collective-permute-start(bf16[40,128]{1,0:T(8,128)(2,1)S(1)} %get-tuple-element.32), channel_id=1, source_target_pairs={{0,8},{1,9},{2,10},{3,11},{4,12},{5,13},{6,14},{7,15},{8,0},{9,1},... | collective-permute-start | bytes 30728 | tf_op jit(solution)/shard_map/ppermute | solution.py:88
  236.8 2.3 collective-permute-start.24
  241.0 5.0 %fusion.6 = bf16[160,3584]{1,0:T(8,128)(2,1)} fusion(f32[160,3584]{1,0:T(8,128)S(1)} %copy-done.7, bf16[256,3584]{1,0:T(8,128)(2,1)} %collective-permute-done.5, bf16[160,3584]{1,0:T(8,128)(2,1)} %collective-permute-done.7, f32[160,256]{1,0:T(8,128)} %fusion.168, bf16[160,3584]{1,0:T(8,128)(2,1)S(1)} %pad_maximum_fusion, ...), kind=kOutput, calls=%fused_computation.12 | convolution fusion | flops 589742080 | bytes 9568256 | tf_op jit(solution)/shard_map/dot_general | solution.py:15
  245.9 1.4 fusion.159
  247.4 2.4 collective-permute-start.8
  251.6 8.4 %collective-permute-done.17 = bf16[160,3584]{1,0:T(8,128)(2,1)} collective-permute-done((bf16[160,3584]{1,0:T(8,128)(2,1)}, bf16[160,3584]{1,0:T(8,128)(2,1)}, u32[]{:S(2)}, u32[]{:S(2)}) %collective-permute-start.17) | collective-permute-done | bytes 1146912 | tf_op jit(solution)/shard_map/ppermute | solution.py:29
  260.1 3.5 %fusion.5 = bf16[160,3584]{1,0:T(8,128)(2,1)S(1)} fusion(f32[160,3584]{1,0:T(8,128)S(1)} %copy-done.8, f32[160,3584]{1,0:T(8,128)} %fusion.69, bf16[3584,256]{1,0:T(8,128)(2,1)} %collective-permute-done.3, bf16[160,3584]{1,0:T(8,128)(2,1)} %collective-permute-done.17, f32[160,256]{1,0:T(8,128)} %copy-done.17, f32[160,256]{1,0:T(8,128)} %copy-done.20, ...), kind=kOutput, calls=%fused_computation.11 | convolution fusion | flops 296878080 | bytes 9207808 | tf_op jit(solution)/shard_map/dot_general | solution.py:19
  263.7 3.2 %collective-permute-start.19 = (bf16[40,3584]{1,0:T(8,128)(2,1)S(1)}, bf16[40,3584]{1,0:T(8,128)(2,1)S(1)}, u32[]{:S(2)}, u32[]{:S(2)}) collective-permute-start(bf16[40,3584]{1,0:T(8,128)(2,1)S(1)} %get-tuple-element.12), channel_id=1, source_target_pairs={{0,8},{1,9},{2,10},{3,11},{4,12},{5,13},{6,14},{7,15},{8,0},{9,1},... | collective-permute-start | bytes 860168 | tf_op jit(solution)/shard_map/ppermute | solution.py:88
  266.8 2.3 collective-permute-start.20
  269.5 18.0 %collective-permute-done.10 = bf16[40,3584]{1,0:T(8,128)(2,1)S(1)} collective-permute-done((bf16[40,3584]{1,0:T(8,128)(2,1)S(1)}, bf16[40,3584]{1,0:T(8,128)(2,1)S(1)}, u32[]{:S(2)}, u32[]{:S(2)}) %collective-permute-start.10) | collective-permute-done | bytes 286752 | tf_op jit(solution)/shard_map/ppermute | solution.py:88
  287.6 1.7 collective-permute-done.18
  289.2 4.5 %collective-permute-done.19 = bf16[40,3584]{1,0:T(8,128)(2,1)S(1)} collective-permute-done((bf16[40,3584]{1,0:T(8,128)(2,1)S(1)}, bf16[40,3584]{1,0:T(8,128)(2,1)S(1)}, u32[]{:S(2)}, u32[]{:S(2)}) %collective-permute-start.19) | collective-permute-done | bytes 286752 | tf_op jit(solution)/shard_map/ppermute | solution.py:88
  293.7 6.1 %collective-permute-done.20 = bf16[40,3584]{1,0:T(8,128)(2,1)S(1)} collective-permute-done((bf16[40,3584]{1,0:T(8,128)(2,1)S(1)}, bf16[40,3584]{1,0:T(8,128)(2,1)S(1)}, u32[]{:S(2)}, u32[]{:S(2)}) %collective-permute-start.20) | collective-permute-done | bytes 286752 | tf_op jit(solution)/shard_map/ppermute | solution.py:88
  299.8 2.7 fusion.20
  (156 shorter events, 36.6 us)
Async XLA Ops:
  0.6 14.1 %copy-start = (bf16[1,3584,4]{1,2,0:T(4,128)(2,1)S(1)}, bf16[1,3584,4]{1,2,0:T(4,128)(2,1)}, u32[]{:S(2)}) copy-start(bf16[1,3584,4]{1,2,0:T(4,128)(2,1)} %param.18) | copy-start | bytes 86020
  0.6 4.5 %copy-start.12 = (bf16[1,64,3584]{2,1,0:T(8,128)(2,1)S(1)}, bf16[1,64,3584]{2,1,0:T(8,128)(2,1)}, u32[]{:S(2)}) copy-start(bf16[1,64,3584]{2,1,0:T(8,128)(2,1)} %param.14) | copy-start | bytes 1376260
  3.6 11.1 %copy-start.26 = (f32[64]{0:T(128)}, f32[64]{0:T(128)S(1)}, u32[]{:S(2)}) copy-start(f32[64]{0:T(128)S(1)} %add_rsqrt_fusion) | copy-start | bytes 772
  5.7 3.6 %copy-start.24 = (s32[1,64,2]{1,2,0:T(2,128)S(1)}, s32[1,64,2]{1,2,0:T(2,128)}, u32[]{:S(2)}) copy-start(s32[1,64,2]{1,2,0:T(2,128)} %param.13) | copy-start | bytes 1540
  5.7 3.8 %copy-start.14 = (bf16[1,64,3584]{2,1,0:T(8,128)(2,1)S(1)}, bf16[1,64,3584]{2,1,0:T(8,128)(2,1)}, u32[]{:S(2)}) copy-start(bf16[1,64,3584]{2,1,0:T(8,128)(2,1)} %param.12) | copy-start | bytes 1376260
  6.9 82.3 %collective-permute-start.12 = (bf16[80,3584]{1,0:T(8,128)(2,1)}, bf16[80,3584]{1,0:T(8,128)(2,1)}, u32[]{:S(2)}, u32[]{:S(2)}) collective-permute-start(bf16[80,3584]{1,0:T(8,128)(2,1)} %get-tuple-element.8), channel_id=1, source_target_pairs={{0,4},{1,5},{2,6},{3,7},{4,8},{5,9},{6,10},{7,11},{8,12},{9,13},{1... | collective-permute-start | bytes 1720328 | tf_op jit(solution)/shard_map/ppermute | solution.py:77
  8.2 83.3 %collective-permute-start.13 = (bf16[80,3584]{1,0:T(8,128)(2,1)}, bf16[80,3584]{1,0:T(8,128)(2,1)}, u32[]{:S(2)}, u32[]{:S(2)}) collective-permute-start(bf16[80,3584]{1,0:T(8,128)(2,1)} %get-tuple-element.9), channel_id=1, source_target_pairs={{0,8},{1,9},{2,10},{3,11},{4,12},{5,13},{6,14},{7,15},{8,0},{9,1},... | collective-permute-start | bytes 1720328 | tf_op jit(solution)/shard_map/ppermute | solution.py:77
  11.2 4.9 %copy-start.23 = (s32[1,64,2]{1,2,0:T(2,128)S(1)}, s32[1,64,2]{1,2,0:T(2,128)}, u32[]{:S(2)}) copy-start(s32[1,64,2]{1,2,0:T(2,128)} %param.16) | copy-start | bytes 1540
  11.2 70.4 %copy-start.1 = (bf16[1,1,3584,256]{3,2,1,0:T(8,128)(2,1)S(1)}, bf16[1,1,3584,256]{3,2,1,0:T(8,128)(2,1)}, u32[]{:S(2)}) copy-start(bf16[1,1,3584,256]{3,2,1,0:T(8,128)(2,1)} %param.20) | copy-start | bytes 5505028
  11.2 64.3 %collective-permute-start = (bf16[40,3584]{1,0:T(8,128)(2,1)}, bf16[40,3584]{1,0:T(8,128)(2,1)}, u32[]{:S(2)}, u32[]{:S(2)}) collective-permute-start(bf16[40,3584]{1,0:T(8,128)(2,1)} %get-tuple-element.22), channel_id=1, source_target_pairs={{0,4},{1,5},{2,6},{3,7},{4,8},{5,9},{6,10},{7,11},{8,12},{9,13},{1... | collective-permute-start | bytes 860168 | tf_op jit(solution)/shard_map/ppermute | solution.py:77
  11.5 70.1 %collective-permute-start.1 = (bf16[40,3584]{1,0:T(8,128)(2,1)}, bf16[40,3584]{1,0:T(8,128)(2,1)}, u32[]{:S(2)}, u32[]{:S(2)}) collective-permute-start(bf16[40,3584]{1,0:T(8,128)(2,1)} %get-tuple-element.21), channel_id=1, source_target_pairs={{0,8},{1,9},{2,10},{3,11},{4,12},{5,13},{6,14},{7,15},{8,0},{9,1},... | collective-permute-start | bytes 860168 | tf_op jit(solution)/shard_map/ppermute | solution.py:77
  14.8 68.1 %collective-permute-start.2 = (bf16[40,3584]{1,0:T(8,128)(2,1)}, bf16[40,3584]{1,0:T(8,128)(2,1)}, u32[]{:S(2)}, u32[]{:S(2)}) collective-permute-start(bf16[40,3584]{1,0:T(8,128)(2,1)} %get-tuple-element.20), channel_id=1, source_target_pairs={{0,12},{1,13},{2,14},{3,15},{4,0},{5,1},{6,2},{7,3},{8,4},{9,5},{1... | collective-permute-start | bytes 860168 | tf_op jit(solution)/shard_map/ppermute | solution.py:77
  16.5 67.9 %copy-start.2 = (bf16[1,1,3584,256]{3,2,1,0:T(8,128)(2,1)S(1)}, bf16[1,1,3584,256]{3,2,1,0:T(8,128)(2,1)}, u32[]{:S(2)}) copy-start(bf16[1,1,3584,256]{3,2,1,0:T(8,128)(2,1)} %param.19) | copy-start | bytes 5505028
  75.5 17.4 %collective-permute-start.14 = (bf16[80,3584]{1,0:T(8,128)(2,1)}, bf16[80,3584]{1,0:T(8,128)(2,1)}, u32[]{:S(2)}, u32[]{:S(2)}) collective-permute-start(bf16[80,3584]{1,0:T(8,128)(2,1)} %get-tuple-element.10), channel_id=1, source_target_pairs={{0,12},{1,13},{2,14},{3,15},{4,0},{5,1},{6,2},{7,3},{8,4},{9,5},{1... | collective-permute-start | bytes 1720328 | tf_op jit(solution)/shard_map/ppermute | solution.py:77
  81.6 88.6 %collective-permute-start.4 = (bf16[3584,256]{1,0:T(8,128)(2,1)S(1)}, bf16[3584,256]{1,0:T(8,128)(2,1)}, u32[]{:S(2)}, u32[]{:S(2)}) collective-permute-start(bf16[3584,256]{1,0:T(8,128)(2,1)S(1)} %bitcast.247), channel_id=1, source_target_pairs={{0,1},{1,0},{2,3},{3,2},{4,5},{5,4},{6,7},{7,6},{8,9},{9,8},{10,11... | collective-permute-start | bytes 5505032 | tf_op jit(solution)/shard_map/ppermute | solution.py:29
  82.8 89.8 %collective-permute-start.3 = (bf16[3584,256]{1,0:T(8,128)(2,1)}, bf16[3584,256]{1,0:T(8,128)(2,1)}, u32[]{:S(2)}, u32[]{:S(2)}) collective-permute-start(bf16[3584,256]{1,0:T(8,128)(2,1)} %bitcast.248), channel_id=1, source_target_pairs={{0,1},{1,0},{2,3},{3,2},{4,5},{5,4},{6,7},{7,6},{8,9},{9,8},{10,11... | collective-permute-start | bytes 5505032 | tf_op jit(solution)/shard_map/ppermute | solution.py:29
  89.2 4.8 %copy-start.18 = (bf16[40,3584]{1,0:T(8,128)(2,1)S(1)}, bf16[40,3584]{1,0:T(8,128)(2,1)}, u32[]{:S(2)}) copy-start(bf16[40,3584]{1,0:T(8,128)(2,1)} %get-tuple-element.23) | copy-start | bytes 860164
  89.2 111.1 %collective-permute-start.5 = (bf16[256,3584]{1,0:T(8,128)(2,1)}, bf16[256,3584]{1,0:T(8,128)(2,1)}, u32[]{:S(2)}, u32[]{:S(2)}) collective-permute-start(bf16[256,3584]{1,0:T(8,128)(2,1)} %bitcast.253), channel_id=1, source_target_pairs={{0,1},{1,0},{2,3},{3,2},{4,5},{5,4},{6,7},{7,6},{8,9},{9,8},{10,11... | collective-permute-start | bytes 5505032 | tf_op jit(solution)/shard_map/ppermute | solution.py:29
  91.5 24.5 %collective-permute-start.6 = (bf16[160,3584]{1,0:T(8,128)(2,1)S(1)}, bf16[160,3584]{1,0:T(8,128)(2,1)S(1)}, u32[]{:S(2)}, u32[]{:S(2)}) collective-permute-start(bf16[160,3584]{1,0:T(8,128)(2,1)S(1)} %pad_maximum_fusion), channel_id=1, source_target_pairs={{0,2},{1,3},{2,0},{3,1},{4,6},{5,7},{6,4},{7,5},{8,10},{9,11},{10,... | collective-permute-start | bytes 3440648 | tf_op jit(solution)/shard_map/ppermute | solution.py:29
  95.1 45.5 %collective-permute-start.16 = (bf16[160,3584]{1,0:T(8,128)(2,1)}, bf16[160,3584]{1,0:T(8,128)(2,1)}, u32[]{:S(2)}, u32[]{:S(2)}) collective-permute-start(bf16[160,3584]{1,0:T(8,128)(2,1)} %pad_maximum_fusion.2), channel_id=1, source_target_pairs={{0,2},{1,3},{2,0},{3,1},{4,6},{5,7},{6,4},{7,5},{8,10},{9,11},{10,... | collective-permute-start | bytes 3440648 | tf_op jit(solution)/shard_map/ppermute | solution.py:29
  98.1 1.9 copy-start.3
  116.0 49.2 %collective-permute-start.15 = (bf16[160,3584]{1,0:T(8,128)(2,1)}, bf16[160,3584]{1,0:T(8,128)(2,1)}, u32[]{:S(2)}, u32[]{:S(2)}) collective-permute-start(bf16[160,3584]{1,0:T(8,128)(2,1)} %pad_maximum_fusion.1), channel_id=1, source_target_pairs={{0,2},{1,3},{2,0},{3,1},{4,6},{5,7},{6,4},{7,5},{8,10},{9,11},{10,... | collective-permute-start | bytes 3440648 | tf_op jit(solution)/shard_map/ppermute | solution.py:29
  122.3 20.1 %copy-start.4 = (bf16[1,1,3584,256]{3,2,1,0:T(8,128)(2,1)S(1)}, bf16[1,1,3584,256]{3,2,1,0:T(8,128)(2,1)}, u32[]{:S(2)}) copy-start(bf16[1,1,3584,256]{3,2,1,0:T(8,128)(2,1)} %param.19) | copy-start | bytes 5505028
  142.4 22.8 %copy-start.11 = (bf16[1,1,256,3584]{3,2,1,0:T(8,128)(2,1)S(1)}, bf16[1,1,256,3584]{3,2,1,0:T(8,128)(2,1)}, u32[]{:S(2)}) copy-start(bf16[1,1,256,3584]{3,2,1,0:T(8,128)(2,1)} %param.21) | copy-start | bytes 5505028
  174.9 29.1 %copy-start.6 = (bf16[160,3584]{1,0:T(8,128)(2,1)S(1)}, bf16[160,3584]{1,0:T(8,128)(2,1)}, u32[]{:S(2)}) copy-start(bf16[160,3584]{1,0:T(8,128)(2,1)} %copy-done.5) | copy-start | bytes 3440644
  203.8 28.9 %collective-permute-start.21 = (bf16[160,128]{1,0:T(8,128)(2,1)}, bf16[160,128]{1,0:T(8,128)(2,1)}, u32[]{:S(2)}, u32[]{:S(2)}) collective-permute-start(bf16[160,128]{1,0:T(8,128)(2,1)} %broadcast_in_dim.40), channel_id=1, source_target_pairs={{0,2},{1,3},{2,0},{3,1},{4,6},{5,7},{6,4},{7,5},{8,10},{9,11},{10,... | collective-permute-start | bytes 122888 | tf_op jit(solution)/shard_map/ppermute | solution.py:29
  211.1 29.8 %collective-permute-start.7 = (bf16[160,3584]{1,0:T(8,128)(2,1)}, bf16[160,3584]{1,0:T(8,128)(2,1)}, u32[]{:S(2)}, u32[]{:S(2)}) collective-permute-start(bf16[160,3584]{1,0:T(8,128)(2,1)} %fusion.7), channel_id=1, source_target_pairs={{0,2},{1,3},{2,0},{3,1},{4,6},{5,7},{6,4},{7,5},{8,10},{9,11},{10,... | collective-permute-start | bytes 3440648 | tf_op jit(solution)/shard_map/ppermute | solution.py:29
  212.4 2.4 copy-start.9
  218.1 41.9 %collective-permute-start.17 = (bf16[160,3584]{1,0:T(8,128)(2,1)}, bf16[160,3584]{1,0:T(8,128)(2,1)}, u32[]{:S(2)}, u32[]{:S(2)}) collective-permute-start(bf16[160,3584]{1,0:T(8,128)(2,1)} %fusion.4), channel_id=1, source_target_pairs={{0,2},{1,3},{2,0},{3,1},{4,6},{5,7},{6,4},{7,5},{8,10},{9,11},{10,... | collective-permute-start | bytes 3440648 | tf_op jit(solution)/shard_map/ppermute | solution.py:29
  220.7 5.4 %copy-start.19 = (f32[160,256]{1,0:T(8,128)}, f32[160,256]{1,0:T(8,128)S(1)}, u32[]{:S(2)}) copy-start(f32[160,256]{1,0:T(8,128)S(1)} %fusion.170) | copy-start | bytes 491524
  223.3 6.5 %copy-start.17 = (f32[160,256]{1,0:T(8,128)}, f32[160,256]{1,0:T(8,128)S(1)}, u32[]{:S(2)}) copy-start(f32[160,256]{1,0:T(8,128)S(1)} %fusion.171) | copy-start | bytes 491524
  226.1 3.8 %copy-start.20 = (f32[160,256]{1,0:T(8,128)}, f32[160,256]{1,0:T(8,128)S(1)}, u32[]{:S(2)}) copy-start(f32[160,256]{1,0:T(8,128)S(1)} %get-tuple-element.51) | copy-start | bytes 491524
  229.9 10.1 %copy-start.21 = (pred[64,2,160]{0,2,1:T(32,128)(4,1)S(1)}, pred[64,2,160]{0,2,1:T(32,128)(4,1)}, u32[]{:S(2)}) copy-start(pred[64,2,160]{0,2,1:T(32,128)(4,1)} %bitcast_and_fusion) | copy-start | bytes 61444
  229.9 11.1 %copy-start.7 = (f32[160,3584]{1,0:T(8,128)S(1)}, f32[160,3584]{1,0:T(8,128)}, u32[]{:S(2)}) copy-start(f32[160,3584]{1,0:T(8,128)} %fusion.66) | copy-start | bytes 6881284
  233.5 5.5 %collective-permute-start.22 = (bf16[40,128]{1,0:T(8,128)(2,1)S(1)}, bf16[40,128]{1,0:T(8,128)(2,1)S(1)}, u32[]{:S(2)}, u32[]{:S(2)}) collective-permute-start(bf16[40,128]{1,0:T(8,128)(2,1)S(1)} %get-tuple-element.33), channel_id=1, source_target_pairs={{0,12},{1,13},{2,14},{3,15},{4,0},{5,1},{6,2},{7,3},{8,4},{9,5},{1... | collective-permute-start | bytes 30728 | tf_op jit(solution)/shard_map/ppermute | solution.py:88
  233.6 5.5 %collective-permute-start.23 = (bf16[40,128]{1,0:T(8,128)(2,1)S(1)}, bf16[40,128]{1,0:T(8,128)(2,1)S(1)}, u32[]{:S(2)}, u32[]{:S(2)}) collective-permute-start(bf16[40,128]{1,0:T(8,128)(2,1)S(1)} %get-tuple-element.32), channel_id=1, source_target_pairs={{0,8},{1,9},{2,10},{3,11},{4,12},{5,13},{6,14},{7,15},{8,0},{9,1},... | collective-permute-start | bytes 30728 | tf_op jit(solution)/shard_map/ppermute | solution.py:88
  236.8 3.1 collective-permute-start.24
  245.9 14.1 %copy-start.8 = (f32[160,3584]{1,0:T(8,128)S(1)}, f32[160,3584]{1,0:T(8,128)}, u32[]{:S(2)}) copy-start(f32[160,3584]{1,0:T(8,128)} %convolution_add_fusion.3) | copy-start | bytes 6881284
  247.4 19.4 %collective-permute-start.8 = (bf16[40,3584]{1,0:T(8,128)(2,1)S(1)}, bf16[40,3584]{1,0:T(8,128)(2,1)S(1)}, u32[]{:S(2)}, u32[]{:S(2)}) collective-permute-start(bf16[40,3584]{1,0:T(8,128)(2,1)S(1)} %get-tuple-element.17), channel_id=1, source_target_pairs={{0,12},{1,13},{2,14},{3,15},{4,0},{5,1},{6,2},{7,3},{8,4},{9,5},{1... | collective-permute-start | bytes 860168 | tf_op jit(solution)/shard_map/ppermute | solution.py:88
  249.8 19.7 %collective-permute-start.9 = (bf16[40,3584]{1,0:T(8,128)(2,1)S(1)}, bf16[40,3584]{1,0:T(8,128)(2,1)S(1)}, u32[]{:S(2)}, u32[]{:S(2)}) collective-permute-start(bf16[40,3584]{1,0:T(8,128)(2,1)S(1)} %get-tuple-element.16), channel_id=1, source_target_pairs={{0,8},{1,9},{2,10},{3,11},{4,12},{5,13},{6,14},{7,15},{8,0},{9,1},... | collective-permute-start | bytes 860168 | tf_op jit(solution)/shard_map/ppermute | solution.py:88
  250.7 36.8 %collective-permute-start.10 = (bf16[40,3584]{1,0:T(8,128)(2,1)S(1)}, bf16[40,3584]{1,0:T(8,128)(2,1)S(1)}, u32[]{:S(2)}, u32[]{:S(2)}) collective-permute-start(bf16[40,3584]{1,0:T(8,128)(2,1)S(1)} %get-tuple-element.15), channel_id=1, source_target_pairs={{0,4},{1,5},{2,6},{3,7},{4,8},{5,9},{6,10},{7,11},{8,12},{9,13},{1... | collective-permute-start | bytes 860168 | tf_op jit(solution)/shard_map/ppermute | solution.py:88
  263.6 25.6 %collective-permute-start.18 = (bf16[40,3584]{1,0:T(8,128)(2,1)S(1)}, bf16[40,3584]{1,0:T(8,128)(2,1)S(1)}, u32[]{:S(2)}, u32[]{:S(2)}) collective-permute-start(bf16[40,3584]{1,0:T(8,128)(2,1)S(1)} %get-tuple-element.13), channel_id=1, source_target_pairs={{0,12},{1,13},{2,14},{3,15},{4,0},{5,1},{6,2},{7,3},{8,4},{9,5},{1... | collective-permute-start | bytes 860168 | tf_op jit(solution)/shard_map/ppermute | solution.py:88
  263.7 30.0 %collective-permute-start.19 = (bf16[40,3584]{1,0:T(8,128)(2,1)S(1)}, bf16[40,3584]{1,0:T(8,128)(2,1)S(1)}, u32[]{:S(2)}, u32[]{:S(2)}) collective-permute-start(bf16[40,3584]{1,0:T(8,128)(2,1)S(1)} %get-tuple-element.12), channel_id=1, source_target_pairs={{0,8},{1,9},{2,10},{3,11},{4,12},{5,13},{6,14},{7,15},{8,0},{9,1},... | collective-permute-start | bytes 860168 | tf_op jit(solution)/shard_map/ppermute | solution.py:88
  266.8 33.0 %collective-permute-start.20 = (bf16[40,3584]{1,0:T(8,128)(2,1)S(1)}, bf16[40,3584]{1,0:T(8,128)(2,1)S(1)}, u32[]{:S(2)}, u32[]{:S(2)}) collective-permute-start(bf16[40,3584]{1,0:T(8,128)(2,1)S(1)} %get-tuple-element.11), channel_id=1, source_target_pairs={{0,4},{1,5},{2,6},{3,7},{4,8},{5,9},{6,10},{7,11},{8,12},{9,13},{1... | collective-permute-start | bytes 860168 | tf_op jit(solution)/shard_map/ppermute | solution.py:88
  299.8 2.7 copy-start.22
  299.8 2.7 copy-start.25
  304.9 2.0 collective-permute-start.25
  306.3 1.9 collective-permute-start.11
  (6 other events, 7.3 us)

commit v2 on v0

v2 whole, which is shorter than its diff:
```python
import functools
import jax
import jax.numpy as jnp
from jax import lax
from jax.experimental import pallas as pl
from jax.experimental.pallas import tpu as pltpu
from jax.sharding import PartitionSpec as P

SPLIT = 4
CHUNKS = 4
LANES = 128
MESH = pl.DeviceIdType.MESH

route_scale = 2.5
norm_eps = 1e-06
last_dims = (((1,), (1,)), ((), ()))


def dot(left, right):
    return jnp.dot(left, right, preferred_element_type=jnp.float32)


def dot_last(left, right):
    return lax.dot_general(left, right, last_dims, preferred_element_type=jnp.float32)


def kernel(
    sizes,
    act_a,
    ids_a,
    idst_a,
    act_b,
    cot_b,
    ids_b,
    idst_b,
    gain,
    router,
    w_gate,
    w_up,
    w_down,
    next_a,
    next_b,
    own_g,
    own_u,
    own_d,
    oth_g,
    oth_u,
    oth_d,
    normed,
    send_a,
    send_b,
    send_c,
    rows_a,
    rows_b,
    rows_c,
    gate_s,
    up_s,
    gact_s,
    mid_a,
    mid_g,
    mid_u,
    near_a,
    near_b,
    ysend_a,
    ysend_b,
    ysend_c,
    yback_a,
    yback_b,
    yback_c,
    zsend_a,
    zsend_b,
    zsend_c,
    home_a,
    home_b,
    home_c,
    grad_n,
    sect_a,
    sect_b,
    load_sem,
    w_send,
    w_recv,
    z_send,
    z_recv,
    y_send,
    y_recv,
    yb_send,
    yb_recv,
    zb_send,
    zb_recv,
    p_send,
    p_recv,
):
    n_expert, n_pipe, experts, slot, top, width, hidden, tokens = sizes
    total_slots = experts * slot
    rows = 2 * total_slots
    cut = width // CHUNKS
    me = lax.axis_index("expert")
    pipe = lax.axis_index("pipe")
    mine = me // SPLIT
    x_dev = {"expert": me + 1 - 2 * (me % 2)}
    y_dev = {"expert": me + 2 - 4 * ((me // 2) % 2)}

    def ahead(step):
        return {"expert": (me + SPLIT * step) % n_expert}

    def behind(step):
        return {"expert": (me + n_expert - SPLIT * step) % n_expert}

    next_pipe = {"pipe": (pipe + 1) % n_pipe}
    last_pipe = {"pipe": (pipe + n_pipe - 1) % n_pipe}

    def remote(src, dst, send, recv, device):
        return pltpu.make_async_remote_copy(
            src_ref=src,
            dst_ref=dst,
            send_sem=send,
            recv_sem=recv,
            device_id=device,
            device_id_type=MESH,
        )

    def columns(n):
        if isinstance(n, int):
            return pl.ds(n * cut, cut)
        return pl.ds(pl.multiple_of(n * cut, cut), cut)

    loads = [
        pltpu.make_async_copy(src, dst, load_sem.at[i])
        for i, (src, dst) in enumerate(((w_gate, own_g), (w_up, own_u), (w_down, own_d)))
    ]
    for load in loads:
        load.start()

    partners = [x_dev, y_dev] + [ahead(step) for step in range(1, experts)] + [next_pipe]
    if n_pipe > 2:
        partners.append(last_pipe)
    barrier = pltpu.get_barrier_semaphore()
    for partner in partners:
        pl.semaphore_signal(barrier, inc=1, device_id=partner, device_id_type=MESH)
    pl.semaphore_wait(barrier, len(partners))

    w_copies = [
        remote(w_gate, oth_g, w_send.at[0], w_recv.at[0], x_dev),
        remote(w_up, oth_u, w_send.at[1], w_recv.at[1], x_dev),
    ]

    def down_copy(n):
        cols = columns(n)
        return remote(
            w_down.at[:, cols], oth_d.at[:, cols], w_send.at[2 + n], w_recv.at[2 + n], x_dev
        )

    for copy in w_copies:
        copy.start()
    for n in range(CHUNKS):
        down_copy(n).start()

    def z_copy(i, send, into, step):
        return remote(
            send.at[step], into.at[0, step], z_send.at[i, step], z_recv.at[i, step], ahead(step)
        )

    def y_copy(i, into, step):
        return remote(
            into.at[0, step], into.at[1, step], y_send.at[i, step], y_recv.at[i, step], y_dev
        )

    def block_of(index):
        count = jnp.zeros_like(index)
        for step in range(1, experts):
            count = count + jnp.where(index >= step * slot, 1, 0)
        place = (index - count * slot).astype(jnp.float32)
        expert = count + mine
        return jnp.where(expert >= experts, expert - experts, expert), place

    gain_row = gain[...].astype(jnp.float32)

    def normalize(act):
        values = act[...].astype(jnp.float32)
        inverse = lax.rsqrt(jnp.mean(values * values, axis=-1, keepdims=True) + norm_eps)
        normed[...] = (values * inverse * gain_row).astype(jnp.bfloat16)
        return inverse

    def route(ids):
        logits = dot_last(normed[...], router[...])
        number = lax.broadcasted_iota(jnp.int32, logits.shape, 1)
        scores = [
            jax.nn.sigmoid(
                jnp.sum(
                    jnp.where(ids[:, k : k + 1] == number, logits, 0.0), axis=1, keepdims=True
                )
            )
            for k in range(top)
        ]
        whole = functools.reduce(lambda a, b: a + b, scores)
        return scores, [score / whole for score in scores], whole

    def pack_mask(idst):
        expert, place = block_of(lax.broadcasted_iota(jnp.int32, (total_slots, tokens), 0))
        named = jnp.zeros((total_slots, tokens), jnp.float32)
        for k in range(top):
            named = named + jnp.where(idst[k : k + 1, :] == expert, 1.0, 0.0)
        first = lax.broadcasted_iota(jnp.int32, (tokens, tokens), 0)
        second = lax.broadcasted_iota(jnp.int32, (tokens, tokens), 1)
        upper = jnp.where(first <= second, 1.0, 0.0).astype(jnp.bfloat16)
        count = dot(named.astype(jnp.bfloat16), upper)
        return jnp.where(count - 1.0 == place, named, 0.0).astype(jnp.bfloat16)

    def unpack_masks(ids):
        expert, place = block_of(lax.broadcasted_iota(jnp.int32, (tokens, total_slots), 1))
        hits = [jnp.where(ids[:, k : k + 1] == expert, 1.0, 0.0) for k in range(top)]
        named = functools.reduce(lambda a, b: a + b, hits)
        first = lax.broadcasted_iota(jnp.int32, (tokens, tokens), 0)
        second = lax.broadcasted_iota(jnp.int32, (tokens, tokens), 1)
        lower = jnp.where(second <= first, 1.0, 0.0).astype(jnp.bfloat16)
        count = dot(lower, named.astype(jnp.bfloat16))
        return [jnp.where(count - 1.0 == place, hit, 0.0).astype(jnp.bfloat16) for hit in hits]

    def pack(i, mask, source, send, into):
        def body(n, carry):
            cols = columns(n)
            packed = dot(mask, source[:, cols]).reshape(experts, slot, cut).astype(jnp.bfloat16)
            send[:, :, cols] = packed
            into[0, 0, :, cols] = packed[0]
            return carry

        lax.fori_loop(0, CHUNKS, body, 0)
        for step in range(1, experts):
            z_copy(i, send, into, step).start()
        y_copy(i, into, 0).start()

    def forward_blocks(i, send, into):
        for step in range(1, experts):
            z_copy(i, send, into, step).wait_recv()
            y_copy(i, into, step).start()

    def arrived(i, into):
        for step in range(experts):
            y_copy(i, into, step).wait_recv()

    inverse_a = normalize(act_a)
    share_a = route(ids_a)[1]
    pack(0, pack_mask(idst_a), normed, send_a, rows_a)
    inverse_b = normalize(act_b)
    mask_b = pack_mask(idst_b)
    pack(1, mask_b, normed, send_b, rows_b)
    pack(2, mask_b, cot_b, send_c, rows_c)
    scores_b, share_b, whole_b = route(ids_b)

    def project(into, gate_w, up_w, half):
        lanes = pl.ds(half * hidden, hidden)

        def body(n, carry):
            cols = columns(n)
            part = into[:, :, :, cols].reshape(rows, cut)
            gate = dot(part, gate_w[cols, :])
            up = dot(part, up_w[cols, :])

            @pl.when(n == 0)
            def _():
                gate_s[:, lanes] = gate
                up_s[:, lanes] = up

            @pl.when(n > 0)
            def _():
                gate_s[:, lanes] += gate
                up_s[:, lanes] += up

            return carry

        lax.fori_loop(0, CHUNKS, body, 0)

    def grad_hidden(n, down_w, half):
        lanes = pl.ds(half * hidden, hidden)
        cols = columns(n)
        part = rows_c[:, :, :, cols].reshape(rows, cut)
        gact_s[:, lanes] += dot_last(part, down_w[:, cols])

    def activate(half):
        lanes = pl.ds(half * hidden, hidden)
        gate = gate_s[:, lanes]
        mid_a[:, lanes] = (gate * jax.nn.sigmoid(gate) * up_s[:, lanes]).astype(jnp.bfloat16)

    forward_blocks(0, send_a, rows_a)
    for load in loads:
        load.wait()
    forward_blocks(1, send_b, rows_b)
    arrived(0, rows_a)
    project(rows_a, own_g, own_u, 0)
    activate(0)
    forward_blocks(2, send_c, rows_c)
    arrived(1, rows_b)
    project(rows_b, own_g, own_u, 0)
    gact_s[...] = jnp.zeros_like(gact_s)
    arrived(2, rows_c)

    def own_grad(n, carry):
        grad_hidden(n, own_d, 0)
        return carry

    lax.fori_loop(0, CHUNKS, own_grad, 0)

    for copy in w_copies:
        copy.wait_recv()
    project(rows_a, oth_g, oth_u, 1)
    activate(1)
    project(rows_b, oth_g, oth_u, 1)

    def yb_copy(i, n, source, into):
        cols = columns(n)
        return remote(
            source.at[:, :, cols], into.at[:, :, cols], yb_send.at[i, n], yb_recv.at[i, n], y_dev
        )

    def zb_copy(i, n, source, into, step):
        cols = columns(n)
        return remote(
            source.at[step, :, cols],
            into.at[step, :, cols],
            zb_send.at[i, n, step],
            zb_recv.at[i, n, step],
            behind(step),
        )

    def split_out(i, n, out, near, source, into):
        cols = columns(n)
        near[:, cols] = out[:total_slots]
        far = out[total_slots:].reshape(experts, slot, cut)
        source[:, :, cols] = far.astype(jnp.bfloat16)
        yb_copy(i, n, source, into).start()

    def join(i, n, near, ysource, yinto, zsource, zinto):
        cols = columns(n)
        yb_copy(i, n, ysource, yinto).wait_recv()
        summed = near[:, cols].reshape(experts, slot, cut) + yinto[:, :, cols].astype(jnp.float32)
        summed = summed.astype(jnp.bfloat16)
        zsource[:, :, cols] = summed
        zinto[0, :, cols] = summed[0]
        for step in range(1, experts):
            zb_copy(i, n, zsource, zinto, step).start()

    def down_step(n):
        cols = columns(n)
        down_copy(n).wait_recv()
        out = dot(mid_a[:, :hidden], own_d[:, cols]) + dot(mid_a[:, hidden:], oth_d[:, cols])
        split_out(0, n, out, near_a, ysend_a, yback_a)
        grad_hidden(n, oth_d, 1)

    def join_a(n):
        join(0, n, near_a, ysend_a, yback_a, zsend_a, home_a)

    def down_loop(n, carry):
        down_step(n)
        join_a(n - 1)
        return carry

    down_step(0)
    lax.fori_loop(1, CHUNKS, down_loop, 0)

    gate = gate_s[...]
    sig = jax.nn.sigmoid(gate)
    up = up_s[...]
    gact = gact_s[...]
    swish = gate * sig
    mid_g[...] = (gact * up * sig * (1.0 + gate * (1.0 - sig))).astype(jnp.bfloat16)
    mid_u[...] = (gact * swish).astype(jnp.bfloat16)
    active = (swish * up).astype(jnp.bfloat16).astype(jnp.float32)
    contract = jnp.broadcast_to(
        jnp.sum(active * gact, axis=-1, keepdims=True), (rows, LANES)
    )
    ysend_c[...] = contract[total_slots:].reshape(experts, slot, LANES).astype(jnp.bfloat16)
    near_c = contract[:total_slots].reshape(experts, slot, LANES)
    yc_copy = remote(ysend_c, yback_c, yb_send.at[1, CHUNKS], yb_recv.at[1, CHUNKS], y_dev)
    yc_copy.start()

    def zc_copy(step):
        return remote(
            zsend_c.at[step],
            home_c.at[step],
            zb_send.at[1, CHUNKS, step],
            zb_recv.at[1, CHUNKS, step],
            behind(step),
        )

    def grad_step(n):
        cols = columns(n)
        out = dot_last(mid_g[:, :hidden], own_g[cols, :])
        out = out + dot_last(mid_u[:, :hidden], own_u[cols, :])
        out = out + dot_last(mid_g[:, hidden:], oth_g[cols, :])
        out = out + dot_last(mid_u[:, hidden:], oth_u[cols, :])
        split_out(1, n, out, near_b, ysend_b, yback_b)

    def join_b(n):
        join(1, n, near_b, ysend_b, yback_b, zsend_b, home_b)

    grad_step(0)
    join_a(CHUNKS - 1)
    yc_copy.wait_recv()
    summed_c = (near_c + yback_c[...].astype(jnp.float32)).astype(jnp.bfloat16)
    zsend_c[...] = summed_c
    home_c[0] = summed_c[0]
    for step in range(1, experts):
        zc_copy(step).start()

    def grad_loop(n, carry):
        grad_step(n)
        join_b(n - 1)
        return carry

    lax.fori_loop(1, CHUNKS, grad_loop, 0)
    join_b(CHUNKS - 1)

    def mix(i, n, zsource, zinto, masks, share):
        cols = columns(n)
        for step in range(1, experts):
            zb_copy(i, n, zsource, zinto, step).wait_recv()
        block = zinto[:, :, cols].reshape(total_slots, cut)
        return functools.reduce(
            lambda a, b: a + b, [share[k] * dot(masks[k], block) for k in range(top)]
        )

    masks_a = unpack_masks(ids_a)

    def finish_a(n, carry):
        cols = columns(n)
        mixed = mix(0, n, zsend_a, home_a, masks_a, share_a)
        values = act_a[:, cols].astype(jnp.float32)
        sect_a[:, cols] = (values + route_scale * mixed).astype(jnp.bfloat16)
        return carry

    lax.fori_loop(0, CHUNKS, finish_a, 0)
    pa_copy = remote(sect_a, next_a, p_send.at[0], p_recv.at[0], next_pipe)
    pa_copy.start()

    masks_b = unpack_masks(ids_b)
    for step in range(1, experts):
        zc_copy(step).wait_recv()
    home = home_c[...].reshape(total_slots, LANES)
    grad_share = [route_scale * dot(masks_b[k], home)[:, :1] for k in range(top)]
    center = functools.reduce(
        lambda a, b: a + b, [share_b[k] * grad_share[k] for k in range(top)]
    )
    number = lax.broadcasted_iota(jnp.int32, (tokens, router.shape[0]), 1)
    dense = jnp.zeros((tokens, router.shape[0]), jnp.float32)
    for k in range(top):
        grad_score = (grad_share[k] - center) / whole_b
        grad_logit = grad_score * scores_b[k] * (1.0 - scores_b[k])
        dense = dense + jnp.where(ids_b[:, k : k + 1] == number, grad_logit, 0.0)
    dense = dense.astype(jnp.bfloat16)

    def finish_b(n, inner):
        cols = columns(n)
        branch = mix(1, n, zsend_b, home_b, masks_b, share_b)
        term = dot(dense, router[:, cols])
        grad = (route_scale * branch + term) * gain[:, cols].astype(jnp.float32)
        grad_n[:, cols] = grad
        values = act_b[:, cols].astype(jnp.float32)
        return inner + jnp.sum(values * grad, axis=-1, keepdims=True)

    inner = lax.fori_loop(0, CHUNKS, finish_b, jnp.zeros((tokens, 1), jnp.float32))
    scale = inverse_b * inverse_b * inverse_b * (inner / width)

    def write_b(n, carry):
        cols = columns(n)
        values = act_b[:, cols].astype(jnp.float32)
        out = cot_b[:, cols].astype(jnp.float32) + inverse_b * grad_n[:, cols] - values * scale
        sect_b[:, cols] = out.astype(jnp.bfloat16)
        return carry

    lax.fori_loop(0, CHUNKS, write_b, 0)
    pb_copy = remote(sect_b, next_b, p_send.at[1], p_recv.at[1], last_pipe)
    pb_copy.start()

    for copy in w_copies:
        copy.wait_send()
    for i, (send, into) in enumerate(((send_a, rows_a), (send_b, rows_b), (send_c, rows_c))):
        y_copy(i, into, 0).wait_send()
        for step in range(1, experts):
            z_copy(i, send, into, step).wait_send()
            y_copy(i, into, step).wait_send()

    def drain(n, carry):
        down_copy(n).wait_send()
        yb_copy(0, n, ysend_a, yback_a).wait_send()
        yb_copy(1, n, ysend_b, yback_b).wait_send()
        for step in range(1, experts):
            zb_copy(0, n, zsend_a, home_a, step).wait_send()
            zb_copy(1, n, zsend_b, home_b, step).wait_send()
        return carry

    lax.fori_loop(0, CHUNKS, drain, 0)
    yc_copy.wait_send()
    for step in range(1, experts):
        zc_copy(step).wait_send()
    pa_copy.wait()
    pb_copy.wait()


def per_device(act_a, ids_a, act_b, cot_b, ids_b, norm_gain, router, w_gate, w_up, w_down):
    n_expert = lax.axis_size("expert")
    n_pipe = lax.axis_size("pipe")
    experts = n_expert // SPLIT
    tokens, width = act_a.shape[1:]
    top = ids_a.shape[2]
    hidden = w_gate.shape[3]
    capacity = min(tokens, max(2, 5 * tokens * top // (4 * experts)))
    slot = -(-capacity // SLOT_ROWS) * SLOT_ROWS
    slots = experts * slot
    rows = 2 * slots
    router_rows = jnp.pad(router[0].T, ((0, max(0, 16 - experts)), (0, 0)))
    sizes = (n_expert, n_pipe, experts, slot, top, width, hidden, tokens)

    def half(*dims):
        return pltpu.VMEM(dims, jnp.bfloat16)

    def full(*dims):
        return pltpu.VMEM(dims, jnp.float32)

    sem = pltpu.SemaphoreType.DMA
    block = (experts, slot, width)
    narrow = (experts, slot, LANES)
    vmem = pl.BlockSpec(memory_space=pltpu.VMEM)
    anywhere = pl.BlockSpec(memory_space=pl.ANY)
    out = jax.ShapeDtypeStruct((tokens, width), jnp.bfloat16)
    next_a, next_b = pl.pallas_call(
        functools.partial(kernel, sizes),
        out_shape=(out, out),
        in_specs=[vmem] * 9 + [anywhere] * 3,
        out_specs=(anywhere, anywhere),
        scratch_shapes=[
            half(width, hidden),
            half(width, hidden),
            half(hidden, width),
            half(width, hidden),
            half(width, hidden),
            half(hidden, width),
            half(tokens, width),
            half(*block),
            half(*block),
            half(*block),
            half(2, *block),
            half(2, *block),
            half(2, *block),
            full(rows, 2 * hidden),
            full(rows, 2 * hidden),
            full(rows, 2 * hidden),
            half(rows, 2 * hidden),
            half(rows, 2 * hidden),
            half(rows, 2 * hidden),
            full(slots, width),
            full(slots, width),
            half(*block),
            half(*block),
            half(*narrow),
            half(*block),
            half(*block),
            half(*narrow),
            half(*block),
            half(*block),
            half(*narrow),
            half(*block),
            half(*block),
            half(*narrow),
            full(tokens, width),
            half(tokens, width),
            half(tokens, width),
            sem((3,)),
            sem((2 + CHUNKS,)),
            sem((2 + CHUNKS,)),
            sem((3, experts)),
            sem((3, experts)),
            sem((3, experts)),
            sem((3, experts)),
            sem((2, CHUNKS + 1)),
            sem((2, CHUNKS + 1)),
            sem((2, CHUNKS + 1, experts)),
            sem((2, CHUNKS + 1, experts)),
            sem((2,)),
            sem((2,)),
        ],
        compiler_params=pltpu.CompilerParams(
            collective_id=0, has_side_effects=True, vmem_limit_bytes=60 * 1024 * 1024
        ),
        cost_estimate=pl.CostEstimate(
            flops=2 * 9 * rows * width * hidden * 2,
            bytes_accessed=6 * width * hidden * 2,
            transcendentals=0,
        ),
    )(
        act_a[0],
        ids_a[0],
        ids_a[0].T,
        act_b[0],
        cot_b[0],
        ids_b[0],
        ids_b[0].T,
        norm_gain,
        router_rows,
        w_gate[0, 0],
        w_up[0, 0],
        w_down[0, 0],
    )
    return (next_a[None], next_b[None])


SLOT_ROWS = 8


def solution(mesh):
    return jax.shard_map(
        per_device,
        mesh=mesh,
        in_specs=(
            P("pipe", "expert", None),
            P("pipe", "expert", None),
            P("pipe", "expert", None),
            P("pipe", "expert", None),
            P("pipe", "expert", None),
            P("pipe", None),
            P("pipe", None, None),
            P("pipe", "expert", None, None),
            P("pipe", "expert", None, None),
            P("pipe", "expert", None, None),
        ),
        out_specs=(P("pipe", "expert", None), P("pipe", "expert", None)),
        check_vma=False,
    )
```

time: 625 us -> 180 us (0.29)
  waiting for transfers between devices: 419 us -> 0 us
  Pallas kernels: 0 us -> 168 us
  local copies, waits for them, and re-layouts: 104 us -> 7.8 us
  matrix products: 40.8 us -> 0 us
  starting transfers between devices: 37.2 us -> 0 us
  other arithmetic: 13.1 us -> 0 us
    all_to_all x6 -> x0, waiting for transfers between devices: 418 us -> none  [the longest x1 91.8 us: per_device(): lax.all_to_all(back_a, 'expert', split_axis=0, concat_axis=0, tiled=True)]
    pallas_call x0 -> x1, Pallas kernels: none -> 168 us  [per_device(): pl.pallas_call(functools.partial(kernel, sizes), out_shape=(out, out), in...]
    scatter x3 -> x0, local copies, waits for them, and re-layouts: 69.1 us -> none  [pack_rows(): buffer = buffer.at[flat_ids, slot_index].set(source[token_rows])]
    dot_general x13 -> x0, matrix products: 40.8 us -> none  [the longest x2 14.6 us: expert_forward(): jnp.dot(activation, down_w, preferred_element_type=jnp.float32)]
    all_to_all x6 -> x0, starting transfers between devices: 33.7 us -> none  [the longest x1 6.74 us: per_device(): lax.all_to_all(send_b, 'expert', split_axis=0, concat_axis=0, tiled=True)]
    gather x6 -> x0, local copies, waits for them, and re-layouts: 16.6 us -> none  [the longest x3 6.16 us: pack_rows(): buffer = buffer.at[flat_ids, slot_index].set(source[token_rows])]
    reduce_sum x13 -> x0, other arithmetic: 9.03 us -> none  [the longest x3 6.12 us: slice_total(): return jnp.sum(shaped.astype(jnp.float32), axis=1)]
    broadcast_in_dim x3 -> x0, local copies, waits for them, and re-layouts: 7.41 us -> none  [pack_rows(): return jnp.repeat(buffer, SPLIT, axis=0)]
  transfers between devices with their start and end apart: 8 -> 0, of which waited for: 6 -> 0; matrix products, arithmetic and copies ran while one was open for 18% -> 0% of each run, Pallas kernels for 0% -> 0%
where the time goes in v2:
time: 180 us; the launch traced here: 176 us
  Pallas kernels  168 us (93%)
  local copies, waits for them, and re-layouts  7.8 us (4%)
    pallas_call x1, Pallas kernels, per_device(): pl.pallas_call(functools.partial(kernel, sizes), out_shape=(out, out), in...  168 us
    unnamed x2, local copies, waits for them, and re-layouts  3.63 us

profile of v2, /device:TPU:13, one launch (start us, length us, event | category | flops | bytes accessed | tf_op | source)
XLA Modules:
  0.0 176.1 jit_solution(1344178895520675989)
XLA Ops:
  0.6 1.4 copy.13.ids_b
  2.0 1.4 copy.12.ids_a
  3.4 1.4 pad.4.router
  4.8 167.7 %shard_map.113 = (bf16[64,3584]{1,0:T(8,128)(2,1)}, bf16[64,3584]{1,0:T(8,128)(2,1)}) custom-call(bf16[64,3584]{1,0:T(8,128)(2,1)} %bitcast.27, s32[64,2]{1,0:T(8,128)} %copy.12.ids_a, s32[2,64]{1,0:T(2,128)} %bitcast.21, bf16[64,3584]{1,0:T(8,128)(2,1)} %bitcast.28, bf16[64,3584]{1,0:T(8,128)(2,1)} %bitcast.29, s32[64,2]{1,0:T(8,128)} %copy.13.ids_b, ...), custom_call_target="tpu_custom_call" | custom-call | flops 10569646080 | bytes 11010048 | tf_op jit(solution)/shard_map/pallas_call | solution.py:525
  172.5 1.8 %copy.16 = bf16[1,64,3584]{2,1,0:T(8,128)(2,1)} copy(bf16[1,64,3584]{2,1,0:T(8,128)(2,1)} %bitcast.18) | data formatting | bytes 917504
  174.3 1.8 %copy.17 = bf16[1,64,3584]{2,1,0:T(8,128)(2,1)} copy(bf16[1,64,3584]{2,1,0:T(8,128)(2,1)} %bitcast.17) | data formatting | bytes 917504

commit v3 on v2

--- a/solution.py
+++ b/solution.py
@@ -7,7 +7,7 @@
 from jax.sharding import PartitionSpec as P
 
 SPLIT = 4
-CHUNKS = 4
+CHUNKS = 7
 LANES = 128
 MESH = pl.DeviceIdType.MESH
 
@@ -26,12 +26,10 @@
 
 def kernel(
     sizes,
-    act_a,
-    ids_a,
+    act_a_hbm,
+    act_b_hbm,
+    cot_b_hbm,
     idst_a,
-    act_b,
-    cot_b,
-    ids_b,
     idst_b,
     gain,
     router,
@@ -46,6 +44,9 @@
     oth_g,
     oth_u,
     oth_d,
+    act_a,
+    act_b,
+    cot_b,
     normed,
     send_a,
     send_b,
@@ -59,16 +60,15 @@
     mid_a,
     mid_g,
     mid_u,
+    mid_x,
     near_a,
-    near_b,
+    part_b,
     ysend_a,
     ysend_b,
     ysend_c,
     yback_a,
     yback_b,
     yback_c,
-    zsend_a,
-    zsend_b,
     zsend_c,
     home_a,
     home_b,
@@ -126,7 +126,16 @@
 
     loads = [
         pltpu.make_async_copy(src, dst, load_sem.at[i])
-        for i, (src, dst) in enumerate(((w_gate, own_g), (w_up, own_u), (w_down, own_d)))
+        for i, (src, dst) in enumerate(
+            (
+                (act_a_hbm, act_a),
+                (act_b_hbm, act_b),
+                (cot_b_hbm, cot_b),
+                (w_gate, own_g),
+                (w_up, own_u),
+                (w_down, own_d),
+            )
+        )
     ]
     for load in loads:
         load.start()
@@ -173,6 +182,18 @@
         expert = count + mine
         return jnp.where(expert >= experts, expert - experts, expert), place
 
+    def ids_columns(idst):
+        first = lax.broadcasted_iota(jnp.int32, (tokens, tokens), 0)
+        second = lax.broadcasted_iota(jnp.int32, (tokens, tokens), 1)
+        return [
+            jnp.sum(
+                jnp.where(first == second, idst[k : k + 1, :].astype(jnp.float32), 0.0),
+                axis=1,
+                keepdims=True,
+            )
+            for k in range(top)
+        ]
+
     gain_row = gain[...].astype(jnp.float32)
 
     def normalize(act):
@@ -183,11 +204,11 @@
 
     def route(ids):
         logits = dot_last(normed[...], router[...])
-        number = lax.broadcasted_iota(jnp.int32, logits.shape, 1)
+        number = lax.broadcasted_iota(jnp.int32, logits.shape, 1).astype(jnp.float32)
         scores = [
             jax.nn.sigmoid(
                 jnp.sum(
-                    jnp.where(ids[:, k : k + 1] == number, logits, 0.0), axis=1, keepdims=True
+                    jnp.where(ids[k] == number, logits, 0.0), axis=1, keepdims=True
                 )
             )
             for k in range(top)
@@ -208,7 +229,8 @@
 
     def unpack_masks(ids):
         expert, place = block_of(lax.broadcasted_iota(jnp.int32, (tokens, total_slots), 1))
-        hits = [jnp.where(ids[:, k : k + 1] == expert, 1.0, 0.0) for k in range(top)]
+        expert = expert.astype(jnp.float32)
+        hits = [jnp.where(ids[k] == expert, 1.0, 0.0) for k in range(top)]
         named = functools.reduce(lambda a, b: a + b, hits)
         first = lax.broadcasted_iota(jnp.int32, (tokens, tokens), 0)
         second = lax.broadcasted_iota(jnp.int32, (tokens, tokens), 1)
@@ -238,6 +260,10 @@
         for step in range(experts):
             y_copy(i, into, step).wait_recv()
 
+    ids_a = ids_columns(idst_a)
+    ids_b = ids_columns(idst_b)
+    for load in loads[:3]:
+        load.wait()
     inverse_a = normalize(act_a)
     share_a = route(ids_a)[1]
     pack(0, pack_mask(idst_a), normed, send_a, rows_a)
@@ -281,16 +307,38 @@
         gate = gate_s[:, lanes]
         mid_a[:, lanes] = (gate * jax.nn.sigmoid(gate) * up_s[:, lanes]).astype(jnp.bfloat16)
 
+    def prepare(half):
+        lanes = pl.ds(half * hidden, hidden)
+        gate = gate_s[:, lanes]
+        up = up_s[:, lanes]
+        sig = jax.nn.sigmoid(gate)
+        swish = gate * sig
+        mid_x[:, lanes] = (swish * up).astype(jnp.bfloat16)
+        gate_s[:, lanes] = up * sig * (1.0 + gate * (1.0 - sig))
+        up_s[:, lanes] = swish
+
+    def finalize(half):
+        lanes = pl.ds(half * hidden, hidden)
+        gact = gact_s[:, lanes]
+        mid_g[:, lanes] = (gact * gate_s[:, lanes]).astype(jnp.bfloat16)
+        mid_u[:, lanes] = (gact * up_s[:, lanes]).astype(jnp.bfloat16)
+        return jnp.sum(mid_x[:, lanes].astype(jnp.float32) * gact, axis=-1, keepdims=True)
+
     forward_blocks(0, send_a, rows_a)
-    for load in loads:
+    for load in loads[3:]:
         load.wait()
     forward_blocks(1, send_b, rows_b)
     arrived(0, rows_a)
     project(rows_a, own_g, own_u, 0)
     activate(0)
     forward_blocks(2, send_c, rows_c)
+    for step in range(1, experts):
+        z_copy(0, send_a, rows_a, step).wait_send()
+        z_copy(1, send_b, rows_b, step).wait_send()
+    zsend_a, zsend_b = send_a, send_b
     arrived(1, rows_b)
     project(rows_b, own_g, own_u, 0)
+    prepare(0)
     gact_s[...] = jnp.zeros_like(gact_s)
     arrived(2, rows_c)
 
@@ -299,12 +347,24 @@
         return carry
 
     lax.fori_loop(0, CHUNKS, own_grad, 0)
+
+    contract_own = finalize(0)
+
+    def own_part(n, carry):
+        cols = columns(n)
+        part_b[:, cols] = dot_last(mid_g[:, :hidden], own_g[cols, :]) + dot_last(
+            mid_u[:, :hidden], own_u[cols, :]
+        )
+        return carry
+
+    lax.fori_loop(0, CHUNKS, own_part, 0)
 
     for copy in w_copies:
         copy.wait_recv()
     project(rows_a, oth_g, oth_u, 1)
     activate(1)
     project(rows_b, oth_g, oth_u, 1)
+    prepare(1)
 
     def yb_copy(i, n, source, into):
         cols = columns(n)
@@ -324,7 +384,7 @@
 
     def split_out(i, n, out, near, source, into):
         cols = columns(n)
-        near[:, cols] = out[:total_slots]
+        near[:total_slots, cols] = out[:total_slots]
         far = out[total_slots:].reshape(experts, slot, cut)
         source[:, :, cols] = far.astype(jnp.bfloat16)
         yb_copy(i, n, source, into).start()
@@ -332,7 +392,8 @@
     def join(i, n, near, ysource, yinto, zsource, zinto):
         cols = columns(n)
         yb_copy(i, n, ysource, yinto).wait_recv()
-        summed = near[:, cols].reshape(experts, slot, cut) + yinto[:, :, cols].astype(jnp.float32)
+        kept = near[:total_slots, cols].reshape(experts, slot, cut)
+        summed = kept + yinto[:, :, cols].astype(jnp.float32)
         summed = summed.astype(jnp.bfloat16)
         zsource[:, :, cols] = summed
         zinto[0, :, cols] = summed[0]
@@ -355,23 +416,14 @@
         return carry
 
     down_step(0)
-    lax.fori_loop(1, CHUNKS, down_loop, 0)
-
-    gate = gate_s[...]
-    sig = jax.nn.sigmoid(gate)
-    up = up_s[...]
-    gact = gact_s[...]
-    swish = gate * sig
-    mid_g[...] = (gact * up * sig * (1.0 + gate * (1.0 - sig))).astype(jnp.bfloat16)
-    mid_u[...] = (gact * swish).astype(jnp.bfloat16)
-    active = (swish * up).astype(jnp.bfloat16).astype(jnp.float32)
+    lax.fori_loop(1, CHUNKS - 1, down_loop, 0)
+    down_step(CHUNKS - 1)
     contract = jnp.broadcast_to(
-        jnp.sum(active * gact, axis=-1, keepdims=True), (rows, LANES)
+        contract_own + finalize(1), (rows, LANES)
     )
     ysend_c[...] = contract[total_slots:].reshape(experts, slot, LANES).astype(jnp.bfloat16)
     near_c = contract[:total_slots].reshape(experts, slot, LANES)
     yc_copy = remote(ysend_c, yback_c, yb_send.at[1, CHUNKS], yb_recv.at[1, CHUNKS], y_dev)
-    yc_copy.start()
 
     def zc_copy(step):
         return remote(
@@ -384,17 +436,20 @@
 
     def grad_step(n):
         cols = columns(n)
-        out = dot_last(mid_g[:, :hidden], own_g[cols, :])
-        out = out + dot_last(mid_u[:, :hidden], own_u[cols, :])
-        out = out + dot_last(mid_g[:, hidden:], oth_g[cols, :])
+        out = dot_last(mid_g[:, hidden:], oth_g[cols, :])
         out = out + dot_last(mid_u[:, hidden:], oth_u[cols, :])
-        split_out(1, n, out, near_b, ysend_b, yback_b)
+        out = out + part_b[:, cols]
+        split_out(1, n, out, part_b, ysend_b, yback_b)
 
     def join_b(n):
-        join(1, n, near_b, ysend_b, yback_b, zsend_b, home_b)
+        join(1, n, part_b, ysend_b, yback_b, zsend_b, home_b)
 
     grad_step(0)
+    yc_copy.start()
+    join_a(CHUNKS - 2)
+    grad_step(1)
     join_a(CHUNKS - 1)
+    join_b(0)
     yc_copy.wait_recv()
     summed_c = (near_c + yback_c[...].astype(jnp.float32)).astype(jnp.bfloat16)
     zsend_c[...] = summed_c
@@ -407,7 +462,7 @@
         join_b(n - 1)
         return carry
 
-    lax.fori_loop(1, CHUNKS, grad_loop, 0)
+    lax.fori_loop(2, CHUNKS, grad_loop, 0)
     join_b(CHUNKS - 1)
 
     def mix(i, n, zsource, zinto, masks, share):
@@ -440,12 +495,12 @@
     center = functools.reduce(
         lambda a, b: a + b, [share_b[k] * grad_share[k] for k in range(top)]
     )
-    number = lax.broadcasted_iota(jnp.int32, (tokens, router.shape[0]), 1)
+    number = lax.broadcasted_iota(jnp.int32, (tokens, router.shape[0]), 1).astype(jnp.float32)
     dense = jnp.zeros((tokens, router.shape[0]), jnp.float32)
     for k in range(top):
         grad_score = (grad_share[k] - center) / whole_b
         grad_logit = grad_score * scores_b[k] * (1.0 - scores_b[k])
-        dense = dense + jnp.where(ids_b[:, k : k + 1] == number, grad_logit, 0.0)
+        dense = dense + jnp.where(ids_b[k] == number, grad_logit, 0.0)
     dense = dense.astype(jnp.bfloat16)
 
     def finish_b(n, inner):
@@ -476,7 +531,8 @@
     for i, (send, into) in enumerate(((send_a, rows_a), (send_b, rows_b), (send_c, rows_c))):
         y_copy(i, into, 0).wait_send()
         for step in range(1, experts):
-            z_copy(i, send, into, step).wait_send()
+            if i == 2:
+                z_copy(i, send, into, step).wait_send()
             y_copy(i, into, step).wait_send()
 
     def drain(n, carry):
@@ -494,6 +550,19 @@
         zc_copy(step).wait_send()
     pa_copy.wait()
     pb_copy.wait()
+
+
+def hand_out(from_a, from_b, into_a, into_b, sems):
+    share = from_a.shape[0] // HAND_PARTS
+    copies = []
+    for i, (src, dst) in enumerate(((from_a, into_a), (from_b, into_b))):
+        for part in range(HAND_PARTS):
+            lines = pl.ds(part * share, share)
+            copies.append(pltpu.make_async_copy(src.at[lines], dst.at[lines], sems.at[i, part]))
+    for copy in copies:
+        copy.start()
+    for copy in copies:
+        copy.wait()
 
 
 def per_device(act_a, ids_a, act_b, cot_b, ids_b, norm_gain, router, w_gate, w_up, w_down):
@@ -507,7 +576,6 @@
     slot = -(-capacity // SLOT_ROWS) * SLOT_ROWS
     slots = experts * slot
     rows = 2 * slots
-    router_rows = jnp.pad(router[0].T, ((0, max(0, 16 - experts)), (0, 0)))
     sizes = (n_expert, n_pipe, experts, slot, top, width, hidden, tokens)
 
     def half(*dims):
@@ -525,7 +593,7 @@
     next_a, next_b = pl.pallas_call(
         functools.partial(kernel, sizes),
         out_shape=(out, out),
-        in_specs=[vmem] * 9 + [anywhere] * 3,
+        in_specs=[anywhere] * 3 + [vmem] * 4 + [anywhere] * 3,
         out_specs=(anywhere, anywhere),
         scratch_shapes=[
             half(width, hidden),
@@ -535,6 +603,9 @@
             half(width, hidden),
             half(hidden, width),
             half(tokens, width),
+            half(tokens, width),
+            half(tokens, width),
+            half(tokens, width),
             half(*block),
             half(*block),
             half(*block),
@@ -547,16 +618,15 @@
             half(rows, 2 * hidden),
             half(rows, 2 * hidden),
             half(rows, 2 * hidden),
+            half(rows, 2 * hidden),
             full(slots, width),
-            full(slots, width),
+            full(rows, width),
             half(*block),
             half(*block),
             half(*narrow),
             half(*block),
             half(*block),
             half(*narrow),
-            half(*block),
-            half(*block),
             half(*narrow),
             half(*block),
             half(*block),
@@ -564,7 +634,7 @@
             full(tokens, width),
             half(tokens, width),
             half(tokens, width),
-            sem((3,)),
+            sem((6,)),
             sem((2 + CHUNKS,)),
             sem((2 + CHUNKS,)),
             sem((3, experts)),
@@ -588,22 +658,28 @@
         ),
     )(
         act_a[0],
-        ids_a[0],
-        ids_a[0].T,
         act_b[0],
         cot_b[0],
-        ids_b[0],
+        ids_a[0].T,
         ids_b[0].T,
         norm_gain,
-        router_rows,
+        router[0].T,
         w_gate[0, 0],
         w_up[0, 0],
         w_down[0, 0],
     )
+    next_a, next_b = pl.pallas_call(
+        hand_out,
+        out_shape=(out, out),
+        in_specs=[anywhere] * 2,
+        out_specs=(anywhere, anywhere),
+        scratch_shapes=[sem((2, HAND_PARTS))],
+    )(next_a, next_b)
     return (next_a[None], next_b[None])
 
 
 SLOT_ROWS = 8
+HAND_PARTS = 4
 
 
 def solution(mesh):

time: 180 us -> 203 us (1.13)
  Pallas kernels: 168 us -> 198 us
  local copies, waits for them, and re-layouts: 7.8 us -> 0 us
    pallas_call x0 -> x1, Pallas kernels: none -> 29 us  [per_device(): pl.pallas_call(hand_out, out_shape=(out, out), in_specs=[anywhere] * 2, o...]
    unnamed x2 -> x0, local copies, waits for them, and re-layouts: 3.63 us -> none
    squeeze x2 -> x0, local copies, waits for them, and re-layouts: 2.76 us -> none  [the longest x1 1.38 us: per_device(): ids_b[0]]
where the time goes in v3:
time: 203 us; the launch traced here: 199 us
  Pallas kernels  198 us (98%)
    pallas_call x1, Pallas kernels, per_device(): pl.pallas_call(functools.partial(kernel, sizes), out_shape=(out, out), in...  169 us
    pallas_call x1, Pallas kernels, per_device(): pl.pallas_call(hand_out, out_shape=(out, out), in_specs=[anywhere] * 2, o...  29 us

profile of v3, /device:TPU:13, one launch (start us, length us, event | category | flops | bytes accessed | tf_op | source)
XLA Modules:
  0.0 199.1 jit_solution(17888690339721709841)
XLA Ops:
  0.6 169.5 %shard_map.113 = (bf16[64,3584]{1,0:T(8,128)(2,1)}, bf16[64,3584]{1,0:T(8,128)(2,1)}) custom-call(bf16[64,3584]{1,0:T(8,128)(2,1)} %bitcast.20, bf16[64,3584]{1,0:T(8,128)(2,1)} %bitcast.21, bf16[64,3584]{1,0:T(8,128)(2,1)} %bitcast.22, s32[2,64]{1,0:T(2,128)} %bitcast.26, s32[2,64]{1,0:T(2,128)} %bitcast.27, bf16[1,3584]{1,0:T(2,128)(2,1)} %gain.1, ...), custom_call_target="tpu_custom_call" | custom-call | flops 10569646080 | bytes 11010048 | tf_op jit(solution)/shard_map/pallas_call | solution.py:593
  170.1 29.0 %shard_map.114 = (bf16[64,3584]{1,0:T(8,128)(2,1)}, bf16[64,3584]{1,0:T(8,128)(2,1)}) custom-call(bf16[64,3584]{1,0:T(8,128)(2,1)} %get-tuple-element.6.from_a, bf16[64,3584]{1,0:T(8,128)(2,1)} %get-tuple-element.7.from_b), custom_call_target="tpu_custom_call" | custom-call | tf_op jit(solution)/shard_map/pallas_call | solution.py:671

commit v4 on v3

--- a/solution.py
+++ b/solution.py
@@ -161,8 +161,6 @@
 
     for copy in w_copies:
         copy.start()
-    for n in range(CHUNKS):
-        down_copy(n).start()
 
     def z_copy(i, send, into, step):
         return remote(
@@ -247,14 +245,16 @@
             return carry
 
         lax.fori_loop(0, CHUNKS, body, 0)
-        for step in range(1, experts):
-            z_copy(i, send, into, step).start()
-        y_copy(i, into, 0).start()
-
-    def forward_blocks(i, send, into):
+
+    def forward_blocks(i, send, into, follow=None):
         for step in range(1, experts):
             z_copy(i, send, into, step).wait_recv()
             y_copy(i, into, step).start()
+            z_copy(i, send, into, step).wait_send()
+            if follow is not None:
+                z_copy(i + 1, *follow, step).start()
+        if follow is not None:
+            y_copy(i + 1, follow[1], 0).start()
 
     def arrived(i, into):
         for step in range(experts):
@@ -267,6 +267,9 @@
     inverse_a = normalize(act_a)
     share_a = route(ids_a)[1]
     pack(0, pack_mask(idst_a), normed, send_a, rows_a)
+    for step in range(1, experts):
+        z_copy(0, send_a, rows_a, step).start()
+    y_copy(0, rows_a, 0).start()
     inverse_b = normalize(act_b)
     mask_b = pack_mask(idst_b)
     pack(1, mask_b, normed, send_b, rows_b)
@@ -324,21 +327,20 @@
         mid_u[:, lanes] = (gact * up_s[:, lanes]).astype(jnp.bfloat16)
         return jnp.sum(mid_x[:, lanes].astype(jnp.float32) * gact, axis=-1, keepdims=True)
 
-    forward_blocks(0, send_a, rows_a)
+    forward_blocks(0, send_a, rows_a, (send_b, rows_b))
     for load in loads[3:]:
         load.wait()
-    forward_blocks(1, send_b, rows_b)
     arrived(0, rows_a)
     project(rows_a, own_g, own_u, 0)
     activate(0)
-    forward_blocks(2, send_c, rows_c)
-    for step in range(1, experts):
-        z_copy(0, send_a, rows_a, step).wait_send()
-        z_copy(1, send_b, rows_b, step).wait_send()
+    forward_blocks(1, send_b, rows_b, (send_c, rows_c))
     zsend_a, zsend_b = send_a, send_b
+    down_copy(0).start()
     arrived(1, rows_b)
     project(rows_b, own_g, own_u, 0)
     prepare(0)
+    forward_blocks(2, send_c, rows_c)
+    down_copy(1).start()
     gact_s[...] = jnp.zeros_like(gact_s)
     arrived(2, rows_c)
 
@@ -403,6 +405,15 @@
     def down_step(n):
         cols = columns(n)
         down_copy(n).wait_recv()
+        if isinstance(n, int):
+            if n + 2 < CHUNKS:
+                down_copy(n + 2).start()
+        else:
+
+            @pl.when(n + 2 < CHUNKS)
+            def _():
+                down_copy(n + 2).start()
+
         out = dot(mid_a[:, :hidden], own_d[:, cols]) + dot(mid_a[:, hidden:], oth_d[:, cols])
         split_out(0, n, out, near_a, ysend_a, yback_a)
         grad_hidden(n, oth_d, 1)
@@ -528,11 +539,8 @@
 
     for copy in w_copies:
         copy.wait_send()
-    for i, (send, into) in enumerate(((send_a, rows_a), (send_b, rows_b), (send_c, rows_c))):
-        y_copy(i, into, 0).wait_send()
-        for step in range(1, experts):
-            if i == 2:
-                z_copy(i, send, into, step).wait_send()
+    for i, into in enumerate((rows_a, rows_b, rows_c)):
+        for step in range(experts):
             y_copy(i, into, step).wait_send()
 
     def drain(n, carry):
@@ -552,17 +560,9 @@
     pb_copy.wait()
 
 
-def hand_out(from_a, from_b, into_a, into_b, sems):
-    share = from_a.shape[0] // HAND_PARTS
-    copies = []
-    for i, (src, dst) in enumerate(((from_a, into_a), (from_b, into_b))):
-        for part in range(HAND_PARTS):
-            lines = pl.ds(part * share, share)
-            copies.append(pltpu.make_async_copy(src.at[lines], dst.at[lines], sems.at[i, part]))
-    for copy in copies:
-        copy.start()
-    for copy in copies:
-        copy.wait()
+def hand_out(from_a, from_b, into_a, into_b):
+    into_a[...] = from_a[...]
+    into_b[...] = from_b[...]
 
 
 def per_device(act_a, ids_a, act_b, cot_b, ids_b, norm_gain, router, w_gate, w_up, w_down):
@@ -671,15 +671,13 @@
     next_a, next_b = pl.pallas_call(
         hand_out,
         out_shape=(out, out),
-        in_specs=[anywhere] * 2,
-        out_specs=(anywhere, anywhere),
-        scratch_shapes=[sem((2, HAND_PARTS))],
+        in_specs=[vmem] * 2,
+        out_specs=(vmem, vmem),
     )(next_a, next_b)
     return (next_a[None], next_b[None])
 
 
 SLOT_ROWS = 8
-HAND_PARTS = 4
 
 
 def solution(mesh):

time: 203 us -> 190 us (0.936)
  Pallas kernels: 198 us -> 185 us
    pallas_call x1, Pallas kernels: 29 us -> 2.11 us  [per_device(): pl.pallas_call(hand_out, out_shape=(out, out), in_specs=[vmem] * 2, out_s...]
    pallas_call x1, Pallas kernels: 169 us -> 183 us  [per_device(): pl.pallas_call(functools.partial(kernel, sizes), out_shape=(out, out), in...]
where the time goes in v4:
time: 190 us; the launch traced here: 186 us
  Pallas kernels  185 us (97%)
    pallas_call x1, Pallas kernels, per_device(): pl.pallas_call(functools.partial(kernel, sizes), out_shape=(out, out), in...  183 us

profile of v4, /device:TPU:13, one launch (start us, length us, event | category | flops | bytes accessed | tf_op | source)
XLA Modules:
  0.0 186.0 jit_solution(1904480684431544250)
XLA Ops:
  0.6 183.2 %shard_map.113 = (bf16[64,3584]{1,0:T(8,128)(2,1)}, bf16[64,3584]{1,0:T(8,128)(2,1)}) custom-call(bf16[64,3584]{1,0:T(8,128)(2,1)} %bitcast.20, bf16[64,3584]{1,0:T(8,128)(2,1)} %bitcast.21, bf16[64,3584]{1,0:T(8,128)(2,1)} %bitcast.22, s32[2,64]{1,0:T(2,128)} %bitcast.26, s32[2,64]{1,0:T(2,128)} %bitcast.27, bf16[1,3584]{1,0:T(2,128)(2,1)} %gain.1, ...), custom_call_target="tpu_custom_call" | custom-call | flops 10569646080 | bytes 11010048 | tf_op jit(solution)/shard_map/pallas_call | solution.py:593
  183.9 2.1 %shard_map.114 = (bf16[64,3584]{1,0:T(8,128)(2,1)}, bf16[64,3584]{1,0:T(8,128)(2,1)}) custom-call(bf16[64,3584]{1,0:T(8,128)(2,1)} %get-tuple-element.6.from_a, bf16[64,3584]{1,0:T(8,128)(2,1)} %get-tuple-element.7.from_b), custom_call_target="tpu_custom_call" | custom-call | tf_op jit(solution)/shard_map/pallas_call | solution.py:671

commit v5 on v4

--- a/solution.py
+++ b/solution.py
@@ -8,6 +8,7 @@
 
 SPLIT = 4
 CHUNKS = 7
+AHEAD = 4
 LANES = 128
 MESH = pl.DeviceIdType.MESH
 
@@ -62,13 +63,15 @@
     mid_u,
     mid_x,
     near_a,
-    part_b,
+    near_b,
     ysend_a,
     ysend_b,
     ysend_c,
     yback_a,
     yback_b,
     yback_c,
+    zsend_a,
+    zsend_b,
     zsend_c,
     home_a,
     home_b,
@@ -246,15 +249,22 @@
 
         lax.fori_loop(0, CHUNKS, body, 0)
 
-    def forward_blocks(i, send, into, follow=None):
+    arrays = ((send_a, rows_a), (send_b, rows_b), (send_c, rows_c))
+    order = [(i, step) for i in range(3) for step in range(1, experts)]
+
+    def start_z(place):
+        if place < len(order):
+            i, step = order[place]
+            z_copy(i, *arrays[i], step).start()
+
+    def forward_blocks(i):
         for step in range(1, experts):
-            z_copy(i, send, into, step).wait_recv()
-            y_copy(i, into, step).start()
-            z_copy(i, send, into, step).wait_send()
-            if follow is not None:
-                z_copy(i + 1, *follow, step).start()
-        if follow is not None:
-            y_copy(i + 1, follow[1], 0).start()
+            z_copy(i, *arrays[i], step).wait_recv()
+            y_copy(i, arrays[i][1], step).start()
+            z_copy(i, *arrays[i], step).wait_send()
+            start_z(order.index((i, step)) + experts)
+        if i < 2:
+            y_copy(i + 1, arrays[i + 1][1], 0).start()
 
     def arrived(i, into):
         for step in range(experts):
@@ -267,12 +277,13 @@
     inverse_a = normalize(act_a)
     share_a = route(ids_a)[1]
     pack(0, pack_mask(idst_a), normed, send_a, rows_a)
-    for step in range(1, experts):
-        z_copy(0, send_a, rows_a, step).start()
+    for place in range(experts - 1):
+        start_z(place)
     y_copy(0, rows_a, 0).start()
     inverse_b = normalize(act_b)
     mask_b = pack_mask(idst_b)
     pack(1, mask_b, normed, send_b, rows_b)
+    start_z(experts - 1)
     pack(2, mask_b, cot_b, send_c, rows_c)
     scores_b, share_b, whole_b = route(ids_b)
 
@@ -327,58 +338,33 @@
         mid_u[:, lanes] = (gact * up_s[:, lanes]).astype(jnp.bfloat16)
         return jnp.sum(mid_x[:, lanes].astype(jnp.float32) * gact, axis=-1, keepdims=True)
 
-    forward_blocks(0, send_a, rows_a, (send_b, rows_b))
+    forward_blocks(0)
     for load in loads[3:]:
         load.wait()
     arrived(0, rows_a)
     project(rows_a, own_g, own_u, 0)
     activate(0)
-    forward_blocks(1, send_b, rows_b, (send_c, rows_c))
-    zsend_a, zsend_b = send_a, send_b
+    forward_blocks(1)
     down_copy(0).start()
     arrived(1, rows_b)
     project(rows_b, own_g, own_u, 0)
     prepare(0)
-    forward_blocks(2, send_c, rows_c)
-    down_copy(1).start()
-    gact_s[...] = jnp.zeros_like(gact_s)
-    arrived(2, rows_c)
-
-    def own_grad(n, carry):
-        grad_hidden(n, own_d, 0)
-        return carry
-
-    lax.fori_loop(0, CHUNKS, own_grad, 0)
-
-    contract_own = finalize(0)
-
-    def own_part(n, carry):
-        cols = columns(n)
-        part_b[:, cols] = dot_last(mid_g[:, :hidden], own_g[cols, :]) + dot_last(
-            mid_u[:, :hidden], own_u[cols, :]
-        )
-        return carry
-
-    lax.fori_loop(0, CHUNKS, own_part, 0)
-
+    forward_blocks(2)
+    for n in range(1, AHEAD):
+        down_copy(n).start()
     for copy in w_copies:
         copy.wait_recv()
     project(rows_a, oth_g, oth_u, 1)
     activate(1)
-    project(rows_b, oth_g, oth_u, 1)
-    prepare(1)
+    gact_s[...] = jnp.zeros_like(gact_s)
 
     def yb_copy(i, n, source, into):
-        cols = columns(n)
+        return remote(source.at[n], into.at[n], yb_send.at[i, n], yb_recv.at[i, n], y_dev)
+
+    def zb_copy(i, n, source, into, step):
         return remote(
-            source.at[:, :, cols], into.at[:, :, cols], yb_send.at[i, n], yb_recv.at[i, n], y_dev
-        )
-
-    def zb_copy(i, n, source, into, step):
-        cols = columns(n)
-        return remote(
-            source.at[step, :, cols],
-            into.at[step, :, cols],
+            source.at[n, step],
+            into.at[n, step],
             zb_send.at[i, n, step],
             zb_recv.at[i, n, step],
             behind(step),
@@ -388,49 +374,56 @@
         cols = columns(n)
         near[:total_slots, cols] = out[:total_slots]
         far = out[total_slots:].reshape(experts, slot, cut)
-        source[:, :, cols] = far.astype(jnp.bfloat16)
+        source[n] = far.astype(jnp.bfloat16)
         yb_copy(i, n, source, into).start()
 
     def join(i, n, near, ysource, yinto, zsource, zinto):
         cols = columns(n)
         yb_copy(i, n, ysource, yinto).wait_recv()
         kept = near[:total_slots, cols].reshape(experts, slot, cut)
-        summed = kept + yinto[:, :, cols].astype(jnp.float32)
+        summed = kept + yinto[n].astype(jnp.float32)
         summed = summed.astype(jnp.bfloat16)
-        zsource[:, :, cols] = summed
-        zinto[0, :, cols] = summed[0]
+        zsource[n] = summed
+        zinto[n, 0] = summed[0]
         for step in range(1, experts):
             zb_copy(i, n, zsource, zinto, step).start()
 
+    def start_down(n):
+        down_copy(n).start()
+
     def down_step(n):
         cols = columns(n)
         down_copy(n).wait_recv()
-        if isinstance(n, int):
-            if n + 2 < CHUNKS:
-                down_copy(n + 2).start()
-        else:
-
-            @pl.when(n + 2 < CHUNKS)
-            def _():
-                down_copy(n + 2).start()
-
+        if not isinstance(n, int):
+            pl.when(n + AHEAD < CHUNKS)(functools.partial(start_down, n + AHEAD))
+        elif n + AHEAD < CHUNKS:
+            start_down(n + AHEAD)
         out = dot(mid_a[:, :hidden], own_d[:, cols]) + dot(mid_a[:, hidden:], oth_d[:, cols])
         split_out(0, n, out, near_a, ysend_a, yback_a)
+
+    def hidden_step(n):
         grad_hidden(n, oth_d, 1)
+        grad_hidden(n, own_d, 0)
 
     def join_a(n):
         join(0, n, near_a, ysend_a, yback_a, zsend_a, home_a)
 
     def down_loop(n, carry):
         down_step(n)
+        hidden_step(n)
         join_a(n - 1)
         return carry
 
     down_step(0)
+    project(rows_b, oth_g, oth_u, 1)
+    prepare(1)
+    arrived(2, rows_c)
+    hidden_step(0)
     lax.fori_loop(1, CHUNKS - 1, down_loop, 0)
     down_step(CHUNKS - 1)
+    hidden_step(CHUNKS - 1)
     contract = jnp.broadcast_to(
-        contract_own + finalize(1), (rows, LANES)
+        finalize(0) + finalize(1), (rows, LANES)
     )
     ysend_c[...] = contract[total_slots:].reshape(experts, slot, LANES).astype(jnp.bfloat16)
     near_c = contract[:total_slots].reshape(experts, slot, LANES)
@@ -449,11 +442,12 @@
         cols = columns(n)
         out = dot_last(mid_g[:, hidden:], oth_g[cols, :])
         out = out + dot_last(mid_u[:, hidden:], oth_u[cols, :])
-        out = out + part_b[:, cols]
-        split_out(1, n, out, part_b, ysend_b, yback_b)
+        out = out + dot_last(mid_g[:, :hidden], own_g[cols, :])
+        out = out + dot_last(mid_u[:, :hidden], own_u[cols, :])
+        split_out(1, n, out, near_b, ysend_b, yback_b)
 
     def join_b(n):
-        join(1, n, part_b, ysend_b, yback_b, zsend_b, home_b)
+        join(1, n, near_b, ysend_b, yback_b, zsend_b, home_b)
 
     grad_step(0)
     yc_copy.start()
@@ -477,10 +471,9 @@
     join_b(CHUNKS - 1)
 
     def mix(i, n, zsource, zinto, masks, share):
-        cols = columns(n)
         for step in range(1, experts):
             zb_copy(i, n, zsource, zinto, step).wait_recv()
-        block = zinto[:, :, cols].reshape(total_slots, cut)
+        block = zinto[n].reshape(total_slots, cut)
         return functools.reduce(
             lambda a, b: a + b, [share[k] * dot(masks[k], block) for k in range(top)]
         )
@@ -587,6 +580,7 @@
     sem = pltpu.SemaphoreType.DMA
     block = (experts, slot, width)
     narrow = (experts, slot, LANES)
+    pieces = (CHUNKS, experts, slot, width // CHUNKS)
     vmem = pl.BlockSpec(memory_space=pltpu.VMEM)
     anywhere = pl.BlockSpec(memory_space=pl.ANY)
     out = jax.ShapeDtypeStruct((tokens, width), jnp.bfloat16)
@@ -620,16 +614,18 @@
             half(rows, 2 * hidden),
             half(rows, 2 * hidden),
             full(slots, width),
-            full(rows, width),
-            half(*block),
-            half(*block),
+            full(slots, width),
+            half(*pieces),
+            half(*pieces),
             half(*narrow),
-            half(*block),
-            half(*block),
+            half(*pieces),
+            half(*pieces),
             half(*narrow),
+            half(*pieces),
+            half(*pieces),
             half(*narrow),
-            half(*block),
-            half(*block),
+            half(*pieces),
+            half(*pieces),
             half(*narrow),
             full(tokens, width),
             half(tokens, width),

time: 190 us -> 169 us (0.89); the launches traced: 186 us -> 167 us
  Pallas kernels: 185 us -> 166 us
    pallas_call x1, Pallas kernels: 183 us -> 164 us  [per_device(): pl.pallas_call(functools.partial(kernel, sizes), out_shape=(out, out), in...]
where the time goes in v5:
time: 169 us; the launch traced here: 167 us
  Pallas kernels  166 us (98%)
    pallas_call x1, Pallas kernels, per_device(): pl.pallas_call(functools.partial(kernel, sizes), out_shape=(out, out), in...  164 us

profile of v5, /device:TPU:13, one launch (start us, length us, event | category | flops | bytes accessed | tf_op | source)
XLA Modules:
  0.0 167.1 jit_solution(14269203227500824529)
XLA Ops:
  0.6 164.4 %shard_map.113 = (bf16[64,3584]{1,0:T(8,128)(2,1)}, bf16[64,3584]{1,0:T(8,128)(2,1)}) custom-call(bf16[64,3584]{1,0:T(8,128)(2,1)} %bitcast.20, bf16[64,3584]{1,0:T(8,128)(2,1)} %bitcast.21, bf16[64,3584]{1,0:T(8,128)(2,1)} %bitcast.22, s32[2,64]{1,0:T(2,128)} %bitcast.26, s32[2,64]{1,0:T(2,128)} %bitcast.27, bf16[1,3584]{1,0:T(2,128)(2,1)} %gain.1, ...), custom_call_target="tpu_custom_call" | custom-call | flops 10569646080 | bytes 11010048 | tf_op jit(solution)/shard_map/pallas_call | solution.py:587
  165.0 2.1 %shard_map.114 = (bf16[64,3584]{1,0:T(8,128)(2,1)}, bf16[64,3584]{1,0:T(8,128)(2,1)}) custom-call(bf16[64,3584]{1,0:T(8,128)(2,1)} %get-tuple-element.6.from_a, bf16[64,3584]{1,0:T(8,128)(2,1)} %get-tuple-element.7.from_b), custom_call_target="tpu_custom_call" | custom-call | tf_op jit(solution)/shard_map/pallas_call | solution.py:667

commit v6 on v5

--- a/solution.py
+++ b/solution.py
@@ -7,8 +7,9 @@
 from jax.sharding import PartitionSpec as P
 
 SPLIT = 4
-CHUNKS = 7
-AHEAD = 4
+CHUNKS = 14
+AHEAD = 8
+PARTS = 7
 LANES = 128
 MESH = pl.DeviceIdType.MESH
 
@@ -97,6 +98,7 @@
     total_slots = experts * slot
     rows = 2 * total_slots
     cut = width // CHUNKS
+    deep = width // PARTS
     me = lax.axis_index("expert")
     pipe = lax.axis_index("pipe")
     mine = me // SPLIT
@@ -126,6 +128,9 @@
         if isinstance(n, int):
             return pl.ds(n * cut, cut)
         return pl.ds(pl.multiple_of(n * cut, cut), cut)
+
+    def wide(n):
+        return pl.ds(pl.multiple_of(n * deep, deep), deep)
 
     loads = [
         pltpu.make_async_copy(src, dst, load_sem.at[i])
@@ -241,13 +246,13 @@
 
     def pack(i, mask, source, send, into):
         def body(n, carry):
-            cols = columns(n)
-            packed = dot(mask, source[:, cols]).reshape(experts, slot, cut).astype(jnp.bfloat16)
+            cols = wide(n)
+            packed = dot(mask, source[:, cols]).reshape(experts, slot, deep).astype(jnp.bfloat16)
             send[:, :, cols] = packed
             into[0, 0, :, cols] = packed[0]
             return carry
 
-        lax.fori_loop(0, CHUNKS, body, 0)
+        lax.fori_loop(0, PARTS, body, 0)
 
     arrays = ((send_a, rows_a), (send_b, rows_b), (send_c, rows_c))
     order = [(i, step) for i in range(3) for step in range(1, experts)]
@@ -291,8 +296,8 @@
         lanes = pl.ds(half * hidden, hidden)
 
         def body(n, carry):
-            cols = columns(n)
-            part = into[:, :, :, cols].reshape(rows, cut)
+            cols = wide(n)
+            part = into[:, :, :, cols].reshape(rows, deep)
             gate = dot(part, gate_w[cols, :])
             up = dot(part, up_w[cols, :])
 
@@ -308,7 +313,7 @@
 
             return carry
 
-        lax.fori_loop(0, CHUNKS, body, 0)
+        lax.fori_loop(0, PARTS, body, 0)
 
     def grad_hidden(n, down_w, half):
         lanes = pl.ds(half * hidden, hidden)
@@ -345,12 +350,13 @@
     project(rows_a, own_g, own_u, 0)
     activate(0)
     forward_blocks(1)
-    down_copy(0).start()
+    for n in range(2):
+        down_copy(n).start()
     arrived(1, rows_b)
     project(rows_b, own_g, own_u, 0)
     prepare(0)
     forward_blocks(2)
-    for n in range(1, AHEAD):
+    for n in range(2, AHEAD):
         down_copy(n).start()
     for copy in w_copies:
         copy.wait_recv()

time: 169 us -> 182 us (1.077)
  Pallas kernels: 166 us -> 181 us
    pallas_call x1, Pallas kernels: 164 us -> 179 us  [per_device(): pl.pallas_call(functools.partial(kernel, sizes), out_shape=(out, out), in...]
where the time goes in v6:
time: 182 us; the launch traced here: 181 us
  Pallas kernels  181 us (99%)
    pallas_call x1, Pallas kernels, per_device(): pl.pallas_call(functools.partial(kernel, sizes), out_shape=(out, out), in...  179 us

profile of v6, /device:TPU:13, one launch (start us, length us, event | category | flops | bytes accessed | tf_op | source)
XLA Modules:
  0.0 181.3 jit_solution(8646406455044628927)
XLA Ops:
  0.6 178.6 %shard_map.113 = (bf16[64,3584]{1,0:T(8,128)(2,1)}, bf16[64,3584]{1,0:T(8,128)(2,1)}) custom-call(bf16[64,3584]{1,0:T(8,128)(2,1)} %bitcast.20, bf16[64,3584]{1,0:T(8,128)(2,1)} %bitcast.21, bf16[64,3584]{1,0:T(8,128)(2,1)} %bitcast.22, s32[2,64]{1,0:T(2,128)} %bitcast.26, s32[2,64]{1,0:T(2,128)} %bitcast.27, bf16[1,3584]{1,0:T(2,128)(2,1)} %gain.1, ...), custom_call_target="tpu_custom_call" | custom-call | flops 10569646080 | bytes 11010048 | tf_op jit(solution)/shard_map/pallas_call | solution.py:593
  179.2 2.1 %shard_map.114 = (bf16[64,3584]{1,0:T(8,128)(2,1)}, bf16[64,3584]{1,0:T(8,128)(2,1)}) custom-call(bf16[64,3584]{1,0:T(8,128)(2,1)} %get-tuple-element.6.from_a, bf16[64,3584]{1,0:T(8,128)(2,1)} %get-tuple-element.7.from_b), custom_call_target="tpu_custom_call" | custom-call | tf_op jit(solution)/shard_map/pallas_call | solution.py:673

commit v7 on v5

--- a/solution.py
+++ b/solution.py
@@ -454,6 +454,7 @@
     join_a(CHUNKS - 2)
     grad_step(1)
     join_a(CHUNKS - 1)
+    grad_step(2)
     join_b(0)
     yc_copy.wait_recv()
     summed_c = (near_c + yback_c[...].astype(jnp.float32)).astype(jnp.bfloat16)
@@ -464,10 +465,11 @@
 
     def grad_loop(n, carry):
         grad_step(n)
-        join_b(n - 1)
+        join_b(n - 2)
         return carry
 
-    lax.fori_loop(2, CHUNKS, grad_loop, 0)
+    lax.fori_loop(3, CHUNKS, grad_loop, 0)
+    join_b(CHUNKS - 2)
     join_b(CHUNKS - 1)
 
     def mix(i, n, zsource, zinto, masks, share):

time: 169 us -> 169 us (level)
  no operation moved by 1% of the time
where the time goes in v7:
time: 169 us; the launch traced here: 167 us
  Pallas kernels  166 us (98%)
    pallas_call x1, Pallas kernels, per_device(): pl.pallas_call(functools.partial(kernel, sizes), out_shape=(out, out), in...  164 us

profile of v7, /device:TPU:13, one launch (start us, length us, event | category | flops | bytes accessed | tf_op | source)
XLA Modules:
  0.0 167.1 jit_solution(968154443914913365)
XLA Ops:
  0.6 164.4 %shard_map.113 = (bf16[64,3584]{1,0:T(8,128)(2,1)}, bf16[64,3584]{1,0:T(8,128)(2,1)}) custom-call(bf16[64,3584]{1,0:T(8,128)(2,1)} %bitcast.20, bf16[64,3584]{1,0:T(8,128)(2,1)} %bitcast.21, bf16[64,3584]{1,0:T(8,128)(2,1)} %bitcast.22, s32[2,64]{1,0:T(2,128)} %bitcast.26, s32[2,64]{1,0:T(2,128)} %bitcast.27, bf16[1,3584]{1,0:T(2,128)(2,1)} %gain.1, ...), custom_call_target="tpu_custom_call" | custom-call | flops 10569646080 | bytes 11010048 | tf_op jit(solution)/shard_map/pallas_call | solution.py:589
  165.0 2.1 %shard_map.114 = (bf16[64,3584]{1,0:T(8,128)(2,1)}, bf16[64,3584]{1,0:T(8,128)(2,1)}) custom-call(bf16[64,3584]{1,0:T(8,128)(2,1)} %get-tuple-element.6.from_a, bf16[64,3584]{1,0:T(8,128)(2,1)} %get-tuple-element.7.from_b), custom_call_target="tpu_custom_call" | custom-call | tf_op jit(solution)/shard_map/pallas_call | solution.py:669
